TPU v7x, 256 devices: a whole 4x4x8 slice. The times are simulated.
256 devices in a mesh: dp: 8 (over y, z_lo), resp: 8 (over x, core), tensor: 4 (over z_hi).
Axes of the slice: x: 4, y: 4, z: 8 (z_hi: 4, z_lo: 2; z = z_hi * 2 + z_lo), core: 2. Of those that a mesh axis runs over, the one named last changes fastest.
Arguments:
- prompt_k: bfloat16 [32768, 512], P(('dp', 'resp', 'tensor')), parts along dimension 0, may hold values from -4 to 4
- prompt_v: bfloat16 [32768, 512], P(('dp', 'resp', 'tensor')), parts along dimension 0, may hold values from -6 to 6
- resp_q: bfloat16 [16384, 2560], P(('dp', 'resp'), 'tensor'), parts along dimension 0, may hold values from -8 to 8
- resp_k: bfloat16 [16384, 512], P(('dp', 'resp'), 'tensor'), parts along dimension 0, may hold values from -6 to 6
- resp_v: bfloat16 [16384, 512], P(('dp', 'resp'), 'tensor'), parts along dimension 0, may hold values from -6 to 6
- resp_grad: bfloat16 [16384, 2560], P(('dp', 'resp'), 'tensor'), parts along dimension 0, may hold values from -6 to 6
- lengths: int32 [64], P(('dp', 'resp')), parts along dimension 0, may hold values from 1 to 256, 1280 in all
Outputs:
- grad_q: float32 [16384, 2560], P(('dp', 'resp'), 'tensor'), parts along dimension 0
- grad_rk: float32 [16384, 512], P(('dp', 'resp'), 'tensor'), parts along dimension 0
- grad_rv: float32 [16384, 512], P(('dp', 'resp'), 'tensor'), parts along dimension 0
- grad_pk: float32 [32768, 512], P(('dp', 'resp', 'tensor')), parts along dimension 0
- grad_pv: float32 [32768, 512], P(('dp', 'resp', 'tensor')), parts along dimension 0
There are 8 independent parts, one for each index of `dp`. A program takes and returns all parts, laid end to end along the dimension named above; each array names one. Nothing has to cross between parts.
Inputs may be any that keep to these rules, and one draw needn't show every extreme that they name: The lengths of one prompt group sum to 1280; the longest fills its buffer.
All inputs are finite; a program needn't handle non-finite values.
Results may differ from a plain program's by a relative error of at most 0.005.
Values may be sent and summed in bfloat16 or wider, within the bound.
A program may use at most 64 MiB of HBM per device.

v0:
```python
import jax
import jax.numpy as jnp
from jax import lax
from jax.sharding import PartitionSpec as P

HD = 128


very_negative = -1e30


def split_keys(block):
    return block.reshape(block.shape[0], block.shape[1] // HD, HD)


def split_query(block, key_width):
    key_heads = key_width // HD
    return block.reshape(block.shape[0], key_heads, block.shape[1] // (key_heads * HD), HD)


def logits(queries, key_rows):
    return jnp.einsum(
        "qhgd,khd->hgqk",
        split_query(queries, key_rows.shape[1]),
        split_keys(key_rows),
        preferred_element_type=jnp.float32,
    ) * HD ** (-0.5)


def fold_stats(state_now, queries, grad_rows, key_rows, val_rows, allowed):
    peak_score, denom_sum, weighted = state_now
    scores = logits(queries, key_rows)
    if allowed is not None:
        scores = jnp.where(allowed[None, None], scores, very_negative)
    new_peak = jnp.maximum(peak_score, jnp.max(scores, axis=3))
    weights_raw = jnp.exp(scores - new_peak[:, :, :, None])
    shrink = jnp.exp(peak_score - new_peak)
    grad_prob = jnp.einsum(
        "qhgd,khd->hgqk",
        split_query(grad_rows, val_rows.shape[1]),
        split_keys(val_rows),
        preferred_element_type=jnp.float32,
    )
    return (
        new_peak,
        denom_sum * shrink + jnp.sum(weights_raw, axis=3),
        weighted * shrink + jnp.sum(weights_raw * grad_prob, axis=3),
    )


def block_grads(queries, grad_rows, log_norm, grad_mean, key_rows, val_rows, allowed):
    key_width = key_rows.shape[1]
    scores = logits(queries, key_rows)
    if allowed is not None:
        scores = jnp.where(allowed[None, None], scores, very_negative)
    prob = jnp.exp(scores - log_norm[:, :, :, None])
    grad_prob = jnp.einsum(
        "qhgd,khd->hgqk",
        split_query(grad_rows, key_width),
        split_keys(val_rows),
        preferred_element_type=jnp.float32,
    )
    dscore_half = (prob * (grad_prob - grad_mean[:, :, :, None])).astype(jnp.bfloat16)
    grad_query = None
    grad_key = None
    grad_val = None
    grad_query = jnp.einsum(
        "hgqk,khd->qhgd", dscore_half, split_keys(key_rows), preferred_element_type=jnp.float32
    ).reshape(queries.shape[0], queries.shape[1])
    prob_half = prob.astype(jnp.bfloat16)
    grad_key = (
        jnp.einsum(
            "hgqk,qhgd->khd",
            dscore_half,
            split_query(queries, key_width),
            preferred_element_type=jnp.float32,
        )
        * HD ** (-0.5)
    ).reshape(-1, key_width)
    grad_val = jnp.einsum(
        "hgqk,qhgd->khd",
        prob_half,
        split_query(grad_rows, key_width),
        preferred_element_type=jnp.float32,
    ).reshape(-1, key_width)
    return (grad_query, grad_key, grad_val)


def local(prompt_k, prompt_v, resp_q, resp_k, resp_v, resp_grad, lengths):
    row_count, feature_width = resp_q.shape
    key_width = resp_k.shape[1]
    key_heads = key_width // HD
    group_size = feature_width // key_width
    positions = lax.broadcasted_iota(jnp.int32, (row_count, 1), 0)
    grad_live = jnp.where(positions < lengths[0], resp_grad, jnp.zeros_like(resp_grad))
    causal = positions >= jnp.transpose(positions)
    mine_k, mine_v = (
        lax.all_to_all(prompt_k, "tensor", split_axis=1, concat_axis=0, tiled=True),
        lax.all_to_all(prompt_v, "tensor", split_axis=1, concat_axis=0, tiled=True),
    )
    full_k, full_v = (
        lax.all_gather(mine_k, "resp", axis=0, tiled=True),
        lax.all_gather(mine_v, "resp", axis=0, tiled=True),
    )
    prompt_rows = full_k.shape[0]
    block_rows = min(512, prompt_rows)
    block_count = prompt_rows // block_rows
    blocks_k = full_k.reshape(block_count, block_rows, key_width)
    blocks_v = full_v.reshape(block_count, block_rows, key_width)
    zero_stats = jnp.zeros((key_heads, group_size, row_count), jnp.float32)
    start_state = (
        jnp.full((key_heads, group_size, row_count), very_negative, jnp.float32),
        zero_stats,
        zero_stats,
    )

    def stats_step(state_now, blocks):
        return (fold_stats(state_now, resp_q, grad_live, blocks[0], blocks[1], None), None)

    state_now, unused = lax.scan(stats_step, start_state, (blocks_k, blocks_v))
    peak_score, denom_sum, weighted = fold_stats(
        state_now, resp_q, grad_live, resp_k, resp_v, causal
    )
    log_norm = peak_score + jnp.log(denom_sum)
    grad_mean = weighted / denom_sum
    own_query, own_key, own_val = block_grads(
        resp_q, grad_live, log_norm, grad_mean, resp_k, resp_v, causal
    )

    def grads_step(partial_value, blocks):
        part_query, part_key, part_val = block_grads(
            resp_q, grad_live, log_norm, grad_mean, blocks[0], blocks[1], None
        )
        return (partial_value + part_query, (part_key, part_val))

    query_sum, terms = lax.scan(grads_step, own_query, (blocks_k, blocks_v))
    share_k, share_v = (
        lax.psum_scatter(
            terms[0].reshape(prompt_rows, key_width), "resp", scatter_dimension=0, tiled=True
        ),
        lax.psum_scatter(
            terms[1].reshape(prompt_rows, key_width), "resp", scatter_dimension=0, tiled=True
        ),
    )
    grad_pk, grad_pv = (
        lax.all_to_all(share_k, "tensor", split_axis=0, concat_axis=1, tiled=True),
        lax.all_to_all(share_v, "tensor", split_axis=0, concat_axis=1, tiled=True),
    )
    grad_q = query_sum * HD ** (-0.5)
    return (grad_q, own_key, own_val, grad_pk, grad_pv)


def solution(mesh):
    in_specs = (
        P(("dp", "resp", "tensor"), None),
        P(("dp", "resp", "tensor"), None),
        P(("dp", "resp"), "tensor"),
        P(("dp", "resp"), "tensor"),
        P(("dp", "resp"), "tensor"),
        P(("dp", "resp"), "tensor"),
        P(("dp", "resp")),
    )
    out_specs = (
        P(("dp", "resp"), "tensor"),
        P(("dp", "resp"), "tensor"),
        P(("dp", "resp"), "tensor"),
        P(("dp", "resp", "tensor"), None),
        P(("dp", "resp", "tensor"), None),
    )
    return jax.shard_map(local, mesh=mesh, in_specs=in_specs, out_specs=out_specs, check_vma=False)
```

profile of v0, /device:TPU:1, one launch (start us, length us, event | category | flops | bytes accessed | tf_op | source)
XLA Modules:
  0.0 254.5 jit_solution(11819209154241257743)
XLA Ops:
  8.5 16.1 %all_to_all.76 = bf16[128,4,128]{2,0,1:T(8,128)(2,1)} all-to-all(bf16[128,4,128]{2,0,1:T(8,128)(2,1)S(1)} %copy.114), channel_id=1, replica_groups=mesh['dp'=8,'resp'=8,'tensor'=4] {'tensor'}, dimensions={1} | all-to-all | bytes 262144 | tf_op jit(solution)/shard_map/all_to_all | solution.py:98
  25.9 10.3 %all_to_all.77 = bf16[128,4,128]{2,0,1:T(8,128)(2,1)} all-to-all(bf16[128,4,128]{2,0,1:T(8,128)(2,1)S(1)} %copy.116), channel_id=1, replica_groups=mesh['dp'=8,'resp'=8,'tensor'=4] {'tensor'}, dimensions={1} | all-to-all | bytes 262144 | tf_op jit(solution)/shard_map/all_to_all | solution.py:99
  38.7 11.5 %all-gather.3.cloned.1.call-done = bf16[4096,128]{1,0:T(8,128)(2,1)} async-done(((bf16[512,128]{1,0:T(8,128)(2,1)}), bf16[4096,128]{1,0:T(8,128)(2,1)}) %all-gather.3.cloned.1.call-update) | async-done | bytes 1048592 | tf_op jit(solution)/shard_map/all_gather | solution.py:102
  50.2 27.7 %all-gather.5.cloned.1.call-done = bf16[4096,128]{1,0:T(8,128)(2,1)} async-done(((bf16[512,128]{1,0:T(8,128)(2,1)}), bf16[4096,128]{1,0:T(8,128)(2,1)}) %all-gather.5.cloned.1.call-update) | async-done | bytes 1048592 | tf_op jit(solution)/shard_map/all_gather | solution.py:103
  77.9 27.9 %while.30 = (s32[]{:T(128)}, f32[1,5,256]{2,1,0:T(8,128)S(1)}, f32[1,5,256]{2,1,0:T(8,128)S(1)}, f32[1,5,256]{2,1,0:T(8,128)S(1)}, bf16[8,512,128]{2,1,0:T(8,128...) while((s32[]{:T(128)}, f32[1,5,256]{2,1,0:T(8,128)S(1)}, ...), condition=%wide.region_4.5_spmd.clone, body=%wide.region_0.4_spmd.clone.sunk | while | flops 341451520 | bytes 8874112 | solution.py:120
  77.9 1.4 bitcast_reduce_fusion.2
  79.3 1.6 fusion.109
  81.4 1.4 bitcast_reduce_fusion.2
  82.8 1.6 fusion.109
  84.9 1.4 bitcast_reduce_fusion.2
  86.3 1.6 fusion.109
  88.3 1.4 bitcast_reduce_fusion.2
  89.8 1.6 fusion.109
  91.8 1.4 bitcast_reduce_fusion.2
  93.3 1.6 fusion.109
  95.3 1.4 bitcast_reduce_fusion.2
  96.7 1.6 fusion.109
  98.8 1.4 bitcast_reduce_fusion.2
  100.2 1.6 fusion.109
  102.3 1.4 bitcast_reduce_fusion.2
  103.7 1.6 fusion.109
  106.8 55.2 %while.29 = (s32[]{:T(128)}, f32[256,640]{0,1:T(8,128)S(1)}, f32[8,512,128]{2,1,0:T(8,128)}, f32[8,512,128]{2,1,0:T(8,128)}, bf16[8,512,128]{2,1,0:T(8,128)(2,1)...) while((s32[]{:T(128)}, f32[256,640]{0,1:T(8,128)S(1)}, ...), condition=%wide.region_9.10_spmd, body=%wide.region_8.9_spmd.sunk | while | flops 844333056 | bytes 16661641 | solution.py:136
  106.8 1.4 fusion.101
  108.2 1.6 fusion.102
  109.8 1.3 fusion.105
  111.1 1.3 fusion.103
  113.7 1.4 fusion.101
  115.1 1.6 fusion.102
  116.7 1.3 fusion.105
  118.0 1.3 fusion.103
  119.4 1.2 fusion.104
  120.6 1.4 fusion.101
  122.0 1.6 fusion.102
  123.6 1.3 fusion.105
  124.9 1.3 fusion.103
  127.5 1.4 fusion.101
  128.9 1.6 fusion.102
  130.5 1.3 fusion.105
  131.8 1.3 fusion.103
  133.2 1.2 fusion.104
  134.4 1.4 fusion.101
  135.8 1.6 fusion.102
  137.4 1.3 fusion.105
  138.7 1.3 fusion.103
  140.1 1.2 fusion.104
  141.3 1.4 fusion.101
  142.7 1.6 fusion.102
  144.3 1.3 fusion.105
  145.6 1.3 fusion.103
  147.0 1.2 fusion.104
  148.2 1.4 fusion.101
  149.6 1.6 fusion.102
  151.2 1.3 fusion.105
  152.5 1.3 fusion.103
  153.9 1.2 fusion.104
  155.1 1.4 fusion.101
  156.5 1.6 fusion.102
  158.1 1.3 fusion.105
  159.4 1.3 fusion.103
  162.6 32.6 %reduce-scatter.3.cloned.1.call-done = f32[512,128]{1,0:T(8,128)} async-done(((f32[4096,128]{1,0:T(8,128)}), f32[512,128]{1,0:T(8,128)}) %reduce-scatter.3.cloned.1.call-update) | async-done | bytes 262160 | tf_op jit(solution)/shard_map/reduce_scatter | solution.py:138
  195.2 6.5 %all-to-all-start.2 = ((f32[4,128,128]{2,1,0:T(8,128)}), f32[4,128,128]{2,1,0:T(8,128)}, u32[]{:S(2)}, u32[]{:S(2)}) async-start(f32[4,128,128]{2,1,0:T(8,128)} %bitcast.333), calls=%async_computation.3 | async-start | bytes 524288 | tf_op jit(solution)/shard_map/all_to_all | solution.py:146
  203.1 29.8 %reduce-scatter.5.cloned.1.call-done = f32[512,128]{1,0:T(8,128)} async-done(((f32[4096,128]{1,0:T(8,128)}), f32[512,128]{1,0:T(8,128)}) %reduce-scatter.5.cloned.1.call-update) | async-done | bytes 262160 | tf_op jit(solution)/shard_map/reduce_scatter | solution.py:141
  232.9 6.2 %all-to-all-start.3 = ((f32[4,128,128]{2,1,0:T(8,128)}), f32[4,128,128]{2,1,0:T(8,128)S(1)}, u32[]{:S(2)}, u32[]{:S(2)}) async-start(f32[4,128,128]{2,1,0:T(8,128)} %bitcast.332), calls=%async_computation.5 | async-start | bytes 524288 | tf_op jit(solution)/shard_map/all_to_all | solution.py:147
  242.9 4.1 %all-to-all-done.3 = f32[4,128,128]{2,1,0:T(8,128)S(1)} async-done(((f32[4,128,128]{2,1,0:T(8,128)}), f32[4,128,128]{2,1,0:T(8,128)S(1)}, u32[]{:S(2)}, u32[]{:S(2)}) %all-to-all-start.3) | async-done | bytes 262176 | tf_op jit(solution)/shard_map/all_to_all | solution.py:147
  (87 shorter events, 20.4 us)
Async XLA Ops:
  7.2 31.2 %copy-start = (bf16[256,128]{1,0:T(8,128)(2,1)S(1)}, bf16[256,128]{1,0:T(8,128)(2,1)}, u32[]{:S(2)}) copy-start(bf16[256,128]{1,0:T(8,128)(2,1)} %param.14) | copy-start | bytes 196612
  7.2 30.9 %copy-start.1 = (bf16[256,640]{1,0:T(8,128)(2,1)S(1)}, bf16[256,640]{1,0:T(8,128)(2,1)}, u32[]{:S(2)}) copy-start(bf16[256,640]{1,0:T(8,128)(2,1)} %param.16) | copy-start | bytes 983044
  7.2 43.0 %all-gather.3.cloned.1.call-start = ((), (), s32[]{:S(2)}) async-start(), calls=%async_computation.6 | async-start | bytes 1179648 | tf_op jit(solution)/shard_map/all_gather | solution.py:102
  24.6 53.2 %all-gather.5.cloned.1.call-start = ((), (), s32[]{:S(2)}) async-start(), calls=%async_computation.7 | async-start | bytes 1179648 | tf_op jit(solution)/shard_map/all_gather | solution.py:103
  36.2 159.0 %reduce-scatter.3.cloned.1.call-start = ((), (), s32[]{:S(2)}) async-start(), calls=%async_computation.8 | async-start | bytes 2359296 | tf_op jit(solution)/shard_map/reduce_scatter | solution.py:138
  77.9 27.9 %copy-start.2 = (bf16[256,128]{1,0:T(8,128)(2,1)S(1)}, bf16[256,128]{1,0:T(8,128)(2,1)}, u32[]{:S(2)}) copy-start(bf16[256,128]{1,0:T(8,128)(2,1)} %param.15) | copy-start | bytes 196612
  162.0 70.8 %reduce-scatter.5.cloned.1.call-start = ((), (), s32[]{:S(2)}) async-start(), calls=%async_computation.9 | async-start | bytes 2359296 | tf_op jit(solution)/shard_map/reduce_scatter | solution.py:141
  195.2 37.7 %all-to-all-start.2 = ((f32[4,128,128]{2,1,0:T(8,128)}), f32[4,128,128]{2,1,0:T(8,128)}, u32[]{:S(2)}, u32[]{:S(2)}) async-start(f32[4,128,128]{2,1,0:T(8,128)} %bitcast.333), calls=%async_computation.3 | async-start | bytes 524288 | tf_op jit(solution)/shard_map/all_to_all | solution.py:146
  232.9 14.2 %all-to-all-start.3 = ((f32[4,128,128]{2,1,0:T(8,128)}), f32[4,128,128]{2,1,0:T(8,128)S(1)}, u32[]{:S(2)}, u32[]{:S(2)}) async-start(f32[4,128,128]{2,1,0:T(8,128)} %bitcast.332), calls=%async_computation.5 | async-start | bytes 524288 | tf_op jit(solution)/shard_map/all_to_all | solution.py:147
Sparse Core Ops, SparseCore 0:
  24.8 25.3 all-gather.2
  52.0 25.7 all-gather.4
  162.1 33.0 reduce-scatter.2
  197.6 35.2 reduce-scatter.4
where the time goes:
time: 259 us; the launch traced here: 255 us
  waiting for transfers between devices  106 us (41%)
  matrix products  80 us (31%)
  blocking collectives  26.4 us (10%)
  between operations  14.6 us (6%)
  starting transfers between devices  12.9 us (5%)
  local copies, waits for them, and re-layouts  7.6 us (3%)
  other arithmetic  6.07 us (2%)
    reduce_scatter x1, waiting for transfers between devices, local(): lax.psum_scatter(terms[0].reshape(prompt_rows, key_width), 'resp', scatte...  32.6 us
    reduce_scatter x1, waiting for transfers between devices, local(): lax.psum_scatter(terms[1].reshape(prompt_rows, key_width), 'resp', scatte...  29.8 us
    all_gather x1, waiting for transfers between devices, local(): lax.all_gather(mine_v, 'resp', axis=0, tiled=True)  27.7 us
    dot_general x17, matrix products, logits(): jnp.einsum('qhgd,khd->hgqk', split_query(queries, key_rows.shape[1]), spl...  22.7 us
    all_to_all x1, blocking collectives, local(): lax.all_to_all(prompt_k, 'tensor', split_axis=1, concat_axis=0, tiled=True)  16.1 us
    dot_general x9, matrix products, block_grads(): jnp.einsum('qhgd,khd->hgqk', split_query(grad_rows, key_width), split_key...  13.1 us
    dot_general x8, matrix products, fold_stats(): jnp.einsum('qhgd,khd->hgqk', split_query(grad_rows, val_rows.shape[1]), s...  12.5 us
    all_gather x1, waiting for transfers between devices, local(): lax.all_gather(mine_k, 'resp', axis=0, tiled=True)  11.5 us
  transfers between devices with their start and end apart: 6, of which 5 were waited for; matrix products, arithmetic and copies ran while one was open for 3% of the time, Pallas kernels for 0%

commit v1 on v0

v1 whole, which is shorter than its diff:
```python
import jax
import jax.numpy as jnp
from jax import lax
from jax.experimental import pallas as pl
from jax.experimental.pallas import tpu as pltpu
from jax.sharding import PartitionSpec as P

HD = 128
SCALE = HD**-0.5
LOG2E = 1.4426950408889634
NEG = -1e30
ROWS = 256
CHUNK = 256

CONTRACT_LAST = (((1,), (1,)), ((), ()))
PLAIN = (((1,), (0,)), ((), ()))


def dot(a, b, dims):
    return lax.dot_general(a, b, dims, preferred_element_type=jnp.float32)


MESH = pl.DeviceIdType.MESH
QUARTER = 128
ROUNDS = 4
TURN = (0, 1, 3, 2)
SPREAD, AHEAD, BEHIND, FAR_K, FAR_V = range(5)

FIRST = ("b0o", "b0t", "d0o", "d0t", "b1o", "b1t", "d1o", "d1t", "b2o", "b2t", "d2o", "d2t", "b3o", "b3t", "d3t", "d3o")
SECOND = ("d3o", "d3t", "b3o", "b3t", "d2o", "d2t", "b2o", "b2t", "d1o", "d1t", "d0o", "d0t", "b1o", "b1t", "b0t", "b0o")


def code(name):
    return (int(name[1]) * 2 + (name[0] == "d")) * 2 + (name[2] == "t")


def pick(step, order):
    chosen = code(order[0])
    for at, name in enumerate(order[1:], 1):
        chosen = jnp.where(step == at, code(name), chosen)
    return chosen // 2, chosen % 2


def attend(base, group, count, keys, vals, causal, qs, lives, peak, denom, weighted, peaks, exps, gprobs):
    for h in range(count):
        at, g = base + h, group + h
        scores = dot(keys, qs[g], CONTRACT_LAST) * (SCALE * LOG2E)
        if causal is not None:
            scores = jnp.where(causal, scores, NEG)
        gprob = dot(vals, lives[g], CONTRACT_LAST)
        scores = scores.reshape(CHUNK // 8, 8, ROWS)
        old = peak[g]
        new = jnp.maximum(old, jnp.max(scores, axis=0))
        raw = jnp.exp2(scores - new[None])
        shrink = jnp.exp2(old - new)
        peak[g] = new
        denom[g] = denom[g] * shrink + jnp.sum(raw, axis=0)
        weighted[g] = weighted[g] * shrink + jnp.sum(raw * gprob.reshape(raw.shape), axis=0)
        peaks[at] = new
        exps[at] = raw.reshape(CHUNK, ROWS)
        gprobs[at] = gprob


def join_sums(group, count, peak, denom, weighted, out):
    for h in range(count):
        top = jnp.max(peak[group + h], axis=0, keepdims=True)
        share = jnp.exp2(peak[group + h] - top)
        out[0, h : h + 1] = top
        out[1, h : h + 1] = jnp.sum(denom[group + h] * share, axis=0, keepdims=True)
        out[2, h : h + 1] = jnp.sum(weighted[group + h] * share, axis=0, keepdims=True)


def finish_stats(group, count, one, two, peak, weighted):
    for h in range(count):
        row = slice(h, h + 1)
        top = jnp.maximum(one[0, row], two[0, row])
        share_one, share_two = jnp.exp2(one[0, row] - top), jnp.exp2(two[0, row] - top)
        total = one[1, row] * share_one + two[1, row] * share_two
        mean = (one[2, row] * share_one + two[2, row] * share_two) / total
        peak[group + h] = jnp.broadcast_to(top + jnp.log2(total), (8, ROWS))
        weighted[group + h] = jnp.broadcast_to(mean, (8, ROWS))


def grads(base, group, count, keys, qs, lives, peak, weighted, peaks, exps, gprobs, dq):
    keys_t = keys.T
    probs, dscores = [], []
    for h in range(count):
        at, g = base + h, group + h
        factor = jnp.exp2(peaks[at] - peak[g])
        prob = exps[at].reshape(CHUNK // 8, 8, ROWS) * factor[None]
        dscore = prob * (gprobs[at].reshape(CHUNK // 8, 8, ROWS) - weighted[g][None])
        probs.append(prob.reshape(CHUNK, ROWS).astype(jnp.bfloat16))
        dscore = dscore.reshape(CHUNK, ROWS).astype(jnp.bfloat16)
        dscores.append(dscore)
        dq[g] += dot(keys_t, dscore, PLAIN)
    rows = pl.ds(group, count)
    grad_v = dot(jnp.concatenate(probs, axis=1), lives[rows].reshape(count * ROWS, HD), PLAIN)
    grad_k = dot(jnp.concatenate(dscores, axis=1), qs[rows].reshape(count * ROWS, HD), PLAIN)
    return grad_k, grad_v


def kernel(lengths, q_hbm, pk_hbm, pv_hbm, rk_hbm, rv_hbm, g_hbm, dq_hbm, drk_hbm, drv_hbm, dpk_hbm, dpv_hbm,
           q, pk, pv, rk, rv, g, dq_out, drk, drv, dpk, dpv,
           qs, lives, peak, denom, weighted, peaks, exps, gprobs, dq, dq_send, dq_in,
           stat_out, stat_in, packed, kv, own, half_out, half_in, ring_out, ring_in, z_out, z_in,
           local_s, swap_s, swap_r, stat_s, stat_r, dq_s, dq_r, get_s, get_r, half_s, half_r, ring_s, ring_r, z_s, z_r):
    heads = q.shape[1] // HD
    resp, tensor = lax.axis_index("resp"), lax.axis_index("tensor")
    chip, core = resp // 2, resp % 2
    up = {"resp": (chip + 1) % 4 * 2 + core}
    down = {"resp": (chip + 3) % 4 * 2 + core}
    twin = {"resp": chip * 2 + 1 - core}

    def along(turn):
        return {"tensor": (tensor + turn) % 4}

    def columns(index):
        return pl.ds(pl.multiple_of(index * HD, HD), HD)

    barrier = pltpu.get_barrier_semaphore()
    for other in (up, down, twin, along(1), along(2), along(3)):
        pl.semaphore_signal(barrier, inc=1, device_id=other, device_id_type=MESH)
    moves_in = [
        pltpu.make_async_copy(src, dst, local_s.at[i])
        for i, (src, dst) in enumerate(
            ((pk_hbm, pk), (pv_hbm, pv), (q_hbm, q), (g_hbm, g), (rk_hbm, rk), (rv_hbm, rv))
        )
    ]
    for move in moves_in:
        move.start()

    def send(src, dst, sems, at, to):
        return pltpu.make_async_remote_copy(
            src_ref=src, dst_ref=dst, send_sem=sems[0].at[at], recv_sem=sems[1].at[at],
            device_id=to, device_id_type=MESH,
        )

    def get(n, kind):
        b, d = 2 * n, 2 * n + 1
        if kind == SPREAD:
            ends = [(packed.at[n, part], kv.at[d, 0, part], along(TURN[n])) for part in range(2)]
        elif kind == AHEAD:
            ends = [(kv.at[d, 0, part], kv.at[b, 0, part], up) for part in range(2)]
        elif kind == BEHIND:
            ends = [(kv.at[d, 0, part], kv.at[b, 1, part], down) for part in range(2)]
        elif kind == FAR_K:
            ends = [(kv.at[b, 0, 0], kv.at[d, 1, 0], up)]
        else:
            ends = [(kv.at[b, 1, 1], kv.at[d, 1, 1], down)]
        return [send(src, dst, (get_s, get_r), (n, kind, i), to) for i, (src, dst, to) in enumerate(ends)]

    def start(copies):
        for copy in copies:
            copy.start()

    def received(copies):
        for copy in copies:
            copy.wait_recv()

    def begin(n):
        if n:
            received(get(n, SPREAD))
        start(get(n, AHEAD))
        start(get(n, BEHIND))

    def forward(n):
        received(get(n, AHEAD))
        start(get(n, FAR_K))
        received(get(n, BEHIND))
        start(get(n, FAR_V))

    def swap():
        return [
            send(ref.at[h], ref.at[heads + h], (swap_s, swap_r), (i, h), twin)
            for h in range(heads)
            for i, ref in enumerate((qs, lives))
        ]

    positions = lax.broadcasted_iota(jnp.int32, (ROWS, HD), 0)
    alive = positions < lengths[0]
    moves_in[0].wait()
    moves_in[1].wait()
    kv[1, 0, 0] = pk[:, columns(tensor)]
    kv[1, 0, 1] = pv[:, columns(tensor)]
    for n in range(1, ROUNDS):
        cols = columns((tensor + TURN[n]) % 4)
        packed[n, 0] = pk[:, cols]
        packed[n, 1] = pv[:, cols]
    pl.semaphore_wait(barrier, 6)
    begin(0)
    for n in range(1, ROUNDS):
        start(get(n, SPREAD))
    moves_in[2].wait()
    moves_in[3].wait()
    for h in range(heads):
        cols = slice(h * HD, (h + 1) * HD)
        qs[h] = q[:, cols]
        lives[h] = jnp.where(alive, g[:, cols], jnp.zeros((), jnp.bfloat16))
    start(swap())
    moves_in[4].wait()
    moves_in[5].wait()
    peak[...] = jnp.full(peak.shape, NEG, jnp.float32)
    denom[...] = jnp.zeros(denom.shape, jnp.float32)
    weighted[...] = jnp.zeros(weighted.shape, jnp.float32)
    dq[...] = jnp.zeros(dq.shape, jnp.float32)
    causal = lax.broadcasted_iota(jnp.int32, (CHUNK, ROWS), 0) <= lax.broadcasted_iota(jnp.int32, (CHUNK, ROWS), 1)
    sums = (qs, lives, peak, denom, weighted, peaks, exps, gprobs)
    steps = len(FIRST)
    attend(steps * heads, 0, heads, rk[...], rv[...], causal, *sums)

    before = {
        "b0o": (lambda: forward(0),),
        "b0t": (lambda: received(swap()),),
        "d0o": (lambda: received(get(0, FAR_K) + get(0, FAR_V)),),
        "d1o": (lambda: received(get(1, FAR_K) + get(1, FAR_V)),),
        "d2o": (lambda: received(get(2, FAR_K) + get(2, FAR_V)),),
        "d3t": (lambda: received(get(3, FAR_K) + get(3, FAR_V)),),
    }
    after = {
        "b0o": (lambda: begin(1),),
        "d0o": (lambda: forward(1),),
        "d0t": (lambda: begin(2),),
        "d1o": (lambda: forward(2), lambda: begin(3)),
        "b2t": (lambda: forward(3),),
    }

    def serve(step, order, table):
        for name, jobs in table.items():
            @pl.when(step == order.index(name))
            def _():
                for job in jobs:
                    job()

    def first(step, carry):
        chunk, half = pick(step, FIRST)
        serve(step, FIRST, before)
        keys = kv[chunk, :, 0].reshape(CHUNK, HD)
        vals = kv[chunk, :, 1].reshape(CHUNK, HD)
        attend((chunk * 2 + half) * heads, half * heads, heads, keys, vals, None, *sums)
        serve(step, FIRST, after)

        @pl.when(step == steps - 2)
        def _():
            join_sums(heads, heads, peak, denom, weighted, stat_out.at[1])
            tell(1).start()

        return carry

    def tell(half):
        return send(stat_out.at[half], stat_in.at[1 - half], (stat_s, stat_r), 1 - half, twin)

    lax.fori_loop(0, steps, first, 0)
    join_sums(0, heads, peak, denom, weighted, stat_out.at[0])
    tell(0).start()
    tell(1).wait_recv()
    finish_stats(0, heads, stat_out.at[0], stat_in.at[0], peak, weighted)

    def to_half(n, part):
        return send(half_out.at[n, part], half_in.at[n, part], (half_s, half_r), (n, part), (up, down)[part])

    def to_ring(n, way):
        return [
            send(ring_out.at[n, way, part], ring_in.at[n, way, part], (ring_s, ring_r), (n, way, part), (up, down)[way])
            for part in range(2)
        ]

    def to_holder(n):
        return [
            send(z_out.at[n, part], z_in.at[n, part], (z_s, z_r), (n, part), along(4 - TURN[n])) for part in range(2)
        ]

    def to_owner(h):
        return send(dq_send.at[h], dq_in.at[h], (dq_s, dq_r), h, twin)

    def wide(ref):
        return ref.astype(jnp.float32)

    def halves(n):
        half_out[n] = own[2 * n + 1, 1].astype(jnp.bfloat16)
        to_half(n, 0).start()
        to_half(n, 1).start()

    def relay(n):
        for way in range(2):
            to_half(n, way).wait_recv()
            part = own[2 * n, 1 - way]
            ring_out[n, way, way] = (part[way] + wide(half_in[n, way])).astype(jnp.bfloat16)
            ring_out[n, way, 1 - way] = part[1 - way].astype(jnp.bfloat16)
            start(to_ring(n, way))

    def total(n):
        received(to_ring(n, 0) + to_ring(n, 1))
        return own[2 * n + 1, 0] + wide(ring_in[n, 0]) + wide(ring_in[n, 1])

    def hand_over(n):
        z_out[n] = total(n).astype(jnp.bfloat16)
        start(to_holder(n))

    def learn():
        tell(0).wait_recv()
        finish_stats(heads, heads, stat_out.at[1], stat_in.at[1], peak, weighted)

    def return_queries():
        for h in range(heads):
            dq_send[h] = dq[heads + h].astype(jnp.bfloat16)
            to_owner(h).start()

    services = {
        "d3o": (learn,),
        "d3t": (lambda: halves(3),),
        "d2o": (lambda: relay(3),),
        "d2t": (lambda: halves(2),),
        "b2t": (lambda: hand_over(3),),
        "d1o": (lambda: relay(2),),
        "d1t": (lambda: halves(1),),
        "d0t": (lambda: halves(0), lambda: hand_over(2)),
        "b1t": (lambda: relay(1),),
        "b0t": (return_queries,),
        "b0o": (lambda: relay(0),),
    }

    def second(step, carry):
        chunk, half = pick(step, SECOND)
        keys = kv[chunk, :, 0].reshape(CHUNK, HD)
        grad_k, grad_v = grads(
            (chunk * 2 + half) * heads, half * heads, heads, keys, qs, lives, peak, weighted, peaks, exps, gprobs, dq
        )
        grad_k = (grad_k * SCALE).reshape(2, QUARTER, HD)
        grad_v = grad_v.reshape(2, QUARTER, HD)
        fresh = step % 2 == 0
        own[chunk, :, 0] = grad_k + jnp.where(fresh, 0.0, own[chunk, :, 0])
        own[chunk, :, 1] = grad_v + jnp.where(fresh, 0.0, own[chunk, :, 1])
        serve(step, SECOND, services)
        return carry

    lax.fori_loop(0, steps, second, 0)
    grad_k, grad_v = grads(steps * heads, 0, heads, rk[...], qs, lives, peak, weighted, peaks, exps, gprobs, dq)
    drk[...] = grad_k * SCALE
    drv[...] = grad_v
    hand_over(1)
    moves_out = [
        pltpu.make_async_copy(src, dst, local_s.at[6 + i])
        for i, (src, dst) in enumerate((
            (drk, drk_hbm), (drv, drv_hbm), (dq_out, dq_hbm), (dpk, dpk_hbm), (dpv, dpv_hbm)
        ))
    ]
    moves_out[0].start()
    moves_out[1].start()
    for h in range(heads):
        to_owner(h).wait_recv()
        dq_out[:, h * HD : (h + 1) * HD] = (dq[h] + wide(dq_in[h])).T * SCALE
    moves_out[2].start()
    sums_now = total(0)
    dpk[:, columns(tensor)] = sums_now[0]
    dpv[:, columns(tensor)] = sums_now[1]
    for n in reversed(range(1, ROUNDS)):
        received(to_holder(n))
        cols = columns((tensor + TURN[n]) % 4)
        dpk[:, cols] = wide(z_in[n, 0])
        dpv[:, cols] = wide(z_in[n, 1])
    moves_out[3].start()
    moves_out[4].start()
    sent = swap() + [tell(0), tell(1)] + [to_owner(h) for h in range(heads)]
    for n in range(ROUNDS):
        for kind in range(SPREAD if n else AHEAD, FAR_V + 1):
            sent += get(n, kind)
        sent += [to_half(n, 0), to_half(n, 1)] + to_ring(n, 0) + to_ring(n, 1)
        if n:
            sent += to_holder(n)
    for copy in sent:
        copy.wait_send()
    for move in moves_out:
        move.wait()


def copy_kernel(*refs):
    sems = refs[-1]
    count = (len(refs) - 1) // 3
    ins, outs, rooms = refs[:count], refs[count : 2 * count], refs[2 * count : 3 * count]
    here = [pltpu.make_async_copy(ins[i], rooms[i], sems.at[0, i]) for i in range(count)]
    away = [pltpu.make_async_copy(rooms[i], outs[i], sems.at[1, i]) for i in range(count)]
    for move in here:
        move.start()
    for i in range(count):
        here[i].wait()
        away[i].start()
    for move in away:
        move.wait()


def local(prompt_k, prompt_v, resp_q, resp_k, resp_v, resp_grad, lengths):
    heads = resp_q.shape[1] // HD
    blocks = (len(FIRST) + 1) * heads
    anywhere = pl.BlockSpec(memory_space=pl.ANY)
    f32, bf16 = jnp.float32, jnp.bfloat16
    stat = pltpu.VMEM((2 * heads, 8, ROWS), f32)
    piece = (2, QUARTER, HD)

    def sems(*shape):
        return [pltpu.SemaphoreType.DMA(shape)] * 2

    outs = tuple(jax.ShapeDtypeStruct(x.shape, f32) for x in (resp_q, resp_k, resp_v, prompt_k, prompt_v))
    flops = 10 * blocks * CHUNK * ROWS * HD
    results = pl.pallas_call(
        kernel,
        out_shape=outs,
        in_specs=[pl.BlockSpec(memory_space=pltpu.SMEM)] + [anywhere] * 6,
        out_specs=[anywhere] * 5,
        scratch_shapes=[
            *(pltpu.VMEM(x.shape, bf16) for x in (resp_q, prompt_k, prompt_v, resp_k, resp_v, resp_grad)),
            *(pltpu.VMEM(x.shape, f32) for x in outs),
            pltpu.VMEM((2 * heads, ROWS, HD), bf16),
            pltpu.VMEM((2 * heads, ROWS, HD), bf16),
            stat,
            stat,
            stat,
            pltpu.VMEM((blocks, 8, ROWS), f32),
            pltpu.VMEM((blocks, CHUNK, ROWS), f32),
            pltpu.VMEM((blocks, CHUNK, ROWS), f32),
            pltpu.VMEM((2 * heads, HD, ROWS), f32),
            pltpu.VMEM((heads, HD, ROWS), bf16),
            pltpu.VMEM((heads, HD, ROWS), bf16),
            pltpu.VMEM((2, 3, 8, ROWS), f32),
            pltpu.VMEM((2, 3, 8, ROWS), f32),
            pltpu.VMEM((ROUNDS,) + piece, bf16),
            pltpu.VMEM((2 * ROUNDS, 2) + piece, bf16),
            pltpu.VMEM((2 * ROUNDS, 2) + piece, f32),
            pltpu.VMEM((ROUNDS,) + piece, bf16),
            pltpu.VMEM((ROUNDS,) + piece, bf16),
            pltpu.VMEM((ROUNDS, 2) + piece, bf16),
            pltpu.VMEM((ROUNDS, 2) + piece, bf16),
            pltpu.VMEM((ROUNDS,) + piece, bf16),
            pltpu.VMEM((ROUNDS,) + piece, bf16),
            pltpu.SemaphoreType.DMA((11,)),
            *sems(2, heads),
            *sems(2),
            *sems(heads),
            *sems(ROUNDS, 5, 2),
            *sems(ROUNDS, 2),
            *sems(ROUNDS, 2, 2),
            *sems(ROUNDS, 2),
        ],
        compiler_params=pltpu.CompilerParams(
            vmem_limit_bytes=61 * 1024 * 1024, collective_id=0, has_side_effects=True
        ),
        cost_estimate=pl.CostEstimate(flops=flops, bytes_accessed=3 << 20, transcendentals=0),
    )(lengths, resp_q, prompt_k, prompt_v, resp_k, resp_v, resp_grad)
    return pl.pallas_call(
        copy_kernel,
        out_shape=outs,
        in_specs=[anywhere] * 5,
        out_specs=[anywhere] * 5,
        scratch_shapes=[pltpu.VMEM(x.shape, f32) for x in outs] + [pltpu.SemaphoreType.DMA((2, 5))],
        compiler_params=pltpu.CompilerParams(vmem_limit_bytes=61 * 1024 * 1024),
    )(*results)


def solution(mesh):
    rows = P(("dp", "resp", "tensor"), None)
    both = P(("dp", "resp"), "tensor")
    return jax.shard_map(
        local,
        mesh=mesh,
        in_specs=(rows, rows, both, both, both, both, P(("dp", "resp"))),
        out_specs=(both, both, both, rows, rows),
        check_vma=False,
    )
```

time: 259 us -> 62.4 us (0.24)
  the two profiles are of different devices: /device:TPU:1 before, /device:TPU:40 now
where the time goes in v1:
time: 62.4 us; the launch traced here: 62.3 us
  Pallas kernels  61 us (98%)
  between operations  1.29 us (2%)
    pallas_call x1, Pallas kernels, local(): pl.pallas_call(kernel, out_shape=outs, in_specs=[pl.BlockSpec(memory_spac...  58.8 us
    pallas_call x1, Pallas kernels, local(): pl.pallas_call(copy_kernel, out_shape=outs, in_specs=[anywhere] * 5, out_...  2.27 us

profile of v1, /device:TPU:40, one launch (start us, length us, event | category | flops | bytes accessed | tf_op | source)
XLA Modules:
  0.0 62.3 jit_solution(16193938707433466735)
XLA Ops:
  1.3 58.8 %shard_map.110 = (f32[256,640]{1,0:T(8,128)}, f32[256,128]{1,0:T(8,128)}, f32[256,128]{1,0:T(8,128)}, f32[128,512]{1,0:T(8,128)}, f32[128,512]{1,0:T(8,128)}) custom-call(s32[1]{0:T(128)S(6)} %copy.12.lengths, bf16[256,640]{1,0:T(8,128)(2,1)} %q_hbm.1, bf16[128,512]{1,0:T(8,128)(2,1)} %pk_hbm.1, bf16[128,512]{1,0:T(8,128)(2,1)} %pv_hbm.1, ...), custom_call_target="tpu_custom_call" | custom-call | flops 7130316800 | bytes 3145728 | tf_op jit(solution)/shard_map/pallas_call | solution.py:404
  60.0 2.3 %shard_map.111 = (f32[256,640]{1,0:T(8,128)}, f32[256,128]{1,0:T(8,128)}, f32[256,128]{1,0:T(8,128)}, f32[128,512]{1,0:T(8,128)}, f32[128,512]{1,0:T(8,128)}) custom-call(f32[256,640]{1,0:T(8,128)} %get-tuple-element.10.refs_0_, f32[256,128]{1,0:T(8,128)} %get-tuple-element.11.refs_1_, f32[256,128]{1,0:T(8,128)} %get-tuple-element.12.refs_2_, ...), custom_call_target="tpu_custom_call" | custom-call | tf_op jit(solution)/shard_map/pallas_call | solution.py:448

commit v2 on v1

--- a/solution.py
+++ b/solution.py
@@ -26,12 +26,17 @@
 TURN = (0, 1, 3, 2)
 SPREAD, AHEAD, BEHIND, FAR_K, FAR_V = range(5)
 
-FIRST = ("b0o", "b0t", "d0o", "d0t", "b1o", "b1t", "d1o", "d1t", "b2o", "b2t", "d2o", "d2t", "b3o", "b3t", "d3t", "d3o")
-SECOND = ("d3o", "d3t", "b3o", "b3t", "d2o", "d2t", "b2o", "b2t", "d1o", "d1t", "d0o", "d0t", "b1o", "b1t", "b0t", "b0o")
+FIRST = ("b0o", "b0t", "c0o", "c0t", "c1o", "c1t", "b1o", "b1t", "b2o", "b2t", "b3t", "d0t", "b3o", "d1t", "d0o", "d1o")
+SECOND = ("d1o", "d0o", "d1t", "d0t", "b3o", "b3t", "b2o", "b2t", "b1o", "b1t", "b0o", "b0t", "c1t", "c1o", "c0t", "c0o")
+BASE = {"b": 0, "c": 4, "d": 6}
 
 
 def code(name):
-    return (int(name[1]) * 2 + (name[0] == "d")) * 2 + (name[2] == "t")
+    return (BASE[name[0]] + int(name[1])) * 2 + (name[2] == "t")
+
+
+def place(letter, n):
+    return BASE[letter] + n // 2, n % 2
 
 
 def pick(step, order):
@@ -136,17 +141,17 @@
         )
 
     def get(n, kind):
-        b, d = 2 * n, 2 * n + 1
+        mine, far = kv.at[*place("c", n)], kv.at[*place("d", n)]
         if kind == SPREAD:
-            ends = [(packed.at[n, part], kv.at[d, 0, part], along(TURN[n])) for part in range(2)]
+            ends = [(packed.at[n, part], mine.at[part], along(TURN[n])) for part in range(2)]
         elif kind == AHEAD:
-            ends = [(kv.at[d, 0, part], kv.at[b, 0, part], up) for part in range(2)]
+            ends = [(mine.at[part], kv.at[n, 0, part], up) for part in range(2)]
         elif kind == BEHIND:
-            ends = [(kv.at[d, 0, part], kv.at[b, 1, part], down) for part in range(2)]
+            ends = [(mine.at[part], kv.at[n, 1, part], down) for part in range(2)]
         elif kind == FAR_K:
-            ends = [(kv.at[b, 0, 0], kv.at[d, 1, 0], up)]
+            ends = [(kv.at[n, 0, 0], far.at[0], up)]
         else:
-            ends = [(kv.at[b, 1, 1], kv.at[d, 1, 1], down)]
+            ends = [(kv.at[n, 1, 1], far.at[1], down)]
         return [send(src, dst, (get_s, get_r), (n, kind, i), to) for i, (src, dst, to) in enumerate(ends)]
 
     def start(copies):
@@ -180,8 +185,8 @@
     alive = positions < lengths[0]
     moves_in[0].wait()
     moves_in[1].wait()
-    kv[1, 0, 0] = pk[:, columns(tensor)]
-    kv[1, 0, 1] = pv[:, columns(tensor)]
+    kv[4, 0, 0] = pk[:, columns(tensor)]
+    kv[4, 0, 1] = pv[:, columns(tensor)]
     for n in range(1, ROUNDS):
         cols = columns((tensor + TURN[n]) % 4)
         packed[n, 0] = pk[:, cols]
@@ -203,24 +208,26 @@
     denom[...] = jnp.zeros(denom.shape, jnp.float32)
     weighted[...] = jnp.zeros(weighted.shape, jnp.float32)
     dq[...] = jnp.zeros(dq.shape, jnp.float32)
+    own[...] = jnp.zeros(own.shape, jnp.float32)
     causal = lax.broadcasted_iota(jnp.int32, (CHUNK, ROWS), 0) <= lax.broadcasted_iota(jnp.int32, (CHUNK, ROWS), 1)
     sums = (qs, lives, peak, denom, weighted, peaks, exps, gprobs)
     steps = len(FIRST)
     attend(steps * heads, 0, heads, rk[...], rv[...], causal, *sums)
 
+    def far_received(*rounds):
+        for n in rounds:
+            received(get(n, FAR_K) + get(n, FAR_V))
+
     before = {
         "b0o": (lambda: forward(0),),
         "b0t": (lambda: received(swap()),),
-        "d0o": (lambda: received(get(0, FAR_K) + get(0, FAR_V)),),
-        "d1o": (lambda: received(get(1, FAR_K) + get(1, FAR_V)),),
-        "d2o": (lambda: received(get(2, FAR_K) + get(2, FAR_V)),),
-        "d3t": (lambda: received(get(3, FAR_K) + get(3, FAR_V)),),
+        "d0t": (lambda: far_received(0, 1),),
+        "d1t": (lambda: far_received(2, 3),),
     }
     after = {
-        "b0o": (lambda: begin(1),),
-        "d0o": (lambda: forward(1),),
-        "d0t": (lambda: begin(2),),
-        "d1o": (lambda: forward(2), lambda: begin(3)),
+        "b0o": (lambda: begin(1), lambda: begin(2)),
+        "c0t": (lambda: begin(3),),
+        "c1t": (lambda: forward(1), lambda: forward(2)),
         "b2t": (lambda: forward(3),),
     }
 
@@ -239,7 +246,7 @@
         attend((chunk * 2 + half) * heads, half * heads, heads, keys, vals, None, *sums)
         serve(step, FIRST, after)
 
-        @pl.when(step == steps - 2)
+        @pl.when(step == FIRST.index("d1t"))
         def _():
             join_sums(heads, heads, peak, denom, weighted, stat_out.at[1])
             tell(1).start()
@@ -276,21 +283,21 @@
         return ref.astype(jnp.float32)
 
     def halves(n):
-        half_out[n] = own[2 * n + 1, 1].astype(jnp.bfloat16)
+        half_out[n] = own[place("d", n)].astype(jnp.bfloat16)
         to_half(n, 0).start()
         to_half(n, 1).start()
 
     def relay(n):
         for way in range(2):
             to_half(n, way).wait_recv()
-            part = own[2 * n, 1 - way]
+            part = own[n, 1 - way]
             ring_out[n, way, way] = (part[way] + wide(half_in[n, way])).astype(jnp.bfloat16)
             ring_out[n, way, 1 - way] = part[1 - way].astype(jnp.bfloat16)
             start(to_ring(n, way))
 
     def total(n):
         received(to_ring(n, 0) + to_ring(n, 1))
-        return own[2 * n + 1, 0] + wide(ring_in[n, 0]) + wide(ring_in[n, 1])
+        return own[place("c", n)] + wide(ring_in[n, 0]) + wide(ring_in[n, 1])
 
     def hand_over(n):
         z_out[n] = total(n).astype(jnp.bfloat16)
@@ -306,17 +313,15 @@
             to_owner(h).start()
 
     services = {
-        "d3o": (learn,),
-        "d3t": (lambda: halves(3),),
-        "d2o": (lambda: relay(3),),
-        "d2t": (lambda: halves(2),),
-        "b2t": (lambda: hand_over(3),),
-        "d1o": (lambda: relay(2),),
-        "d1t": (lambda: halves(1),),
-        "d0t": (lambda: halves(0), lambda: hand_over(2)),
+        "d0o": (learn,),
+        "d1t": (lambda: halves(3), lambda: halves(2)),
+        "d0t": (lambda: halves(1), lambda: halves(0)),
+        "b2t": (lambda: relay(3), lambda: relay(2)),
         "b1t": (lambda: relay(1),),
-        "b0t": (return_queries,),
-        "b0o": (lambda: relay(0),),
+        "b0t": (lambda: relay(0),),
+        "c1o": (lambda: hand_over(3), lambda: hand_over(2)),
+        "c0t": (return_queries,),
+        "c0o": (lambda: hand_over(1),),
     }
 
     def second(step, carry):
@@ -327,9 +332,8 @@
         )
         grad_k = (grad_k * SCALE).reshape(2, QUARTER, HD)
         grad_v = grad_v.reshape(2, QUARTER, HD)
-        fresh = step % 2 == 0
-        own[chunk, :, 0] = grad_k + jnp.where(fresh, 0.0, own[chunk, :, 0])
-        own[chunk, :, 1] = grad_v + jnp.where(fresh, 0.0, own[chunk, :, 1])
+        own[chunk, :, 0] += grad_k
+        own[chunk, :, 1] += grad_v
         serve(step, SECOND, services)
         return carry
 
@@ -337,7 +341,6 @@
     grad_k, grad_v = grads(steps * heads, 0, heads, rk[...], qs, lives, peak, weighted, peaks, exps, gprobs, dq)
     drk[...] = grad_k * SCALE
     drv[...] = grad_v
-    hand_over(1)
     moves_out = [
         pltpu.make_async_copy(src, dst, local_s.at[6 + i])
         for i, (src, dst) in enumerate((

time: 62.4 us -> 54.4 us (0.87)
  the two profiles are of different devices: /device:TPU:40 before, /device:TPU:1 now
where the time goes in v2:
time: 54.4 us; the launch traced here: 54.3 us
  Pallas kernels  53 us (97%)
  between operations  1.29 us (2%)
    pallas_call x1, Pallas kernels, local(): pl.pallas_call(kernel, out_shape=outs, in_specs=[pl.BlockSpec(memory_spac...  50.7 us
    pallas_call x1, Pallas kernels, local(): pl.pallas_call(copy_kernel, out_shape=outs, in_specs=[anywhere] * 5, out_...  2.27 us

profile of v2, /device:TPU:1, one launch (start us, length us, event | category | flops | bytes accessed | tf_op | source)
XLA Modules:
  0.0 54.3 jit_solution(4102421626435832903)
XLA Ops:
  1.3 50.7 %shard_map.110 = (f32[256,640]{1,0:T(8,128)}, f32[256,128]{1,0:T(8,128)}, f32[256,128]{1,0:T(8,128)}, f32[128,512]{1,0:T(8,128)}, f32[128,512]{1,0:T(8,128)}) custom-call(s32[1]{0:T(128)S(6)} %copy.12.lengths, bf16[256,640]{1,0:T(8,128)(2,1)} %q_hbm.1, bf16[128,512]{1,0:T(8,128)(2,1)} %pk_hbm.1, bf16[128,512]{1,0:T(8,128)(2,1)} %pv_hbm.1, ...), custom_call_target="tpu_custom_call" | custom-call | flops 7130316800 | bytes 3145728 | tf_op jit(solution)/shard_map/pallas_call | solution.py:407
  52.0 2.3 %shard_map.111 = (f32[256,640]{1,0:T(8,128)}, f32[256,128]{1,0:T(8,128)}, f32[256,128]{1,0:T(8,128)}, f32[128,512]{1,0:T(8,128)}, f32[128,512]{1,0:T(8,128)}) custom-call(f32[256,640]{1,0:T(8,128)} %get-tuple-element.10.refs_0_, f32[256,128]{1,0:T(8,128)} %get-tuple-element.11.refs_1_, f32[256,128]{1,0:T(8,128)} %get-tuple-element.12.refs_2_, ...), custom_call_target="tpu_custom_call" | custom-call | tf_op jit(solution)/shard_map/pallas_call | solution.py:451

commit v3 on v2

--- a/solution.py
+++ b/solution.py
@@ -24,26 +24,27 @@
 QUARTER = 128
 ROUNDS = 4
 TURN = (0, 1, 3, 2)
-SPREAD, AHEAD, BEHIND, FAR_K, FAR_V = range(5)
-
-FIRST = ("b0o", "b0t", "c0o", "c0t", "c1o", "c1t", "b1o", "b1t", "b2o", "b2t", "b3t", "d0t", "b3o", "d1t", "d0o", "d1o")
-SECOND = ("d1o", "d0o", "d1t", "d0t", "b3o", "b3t", "b2o", "b2t", "b1o", "b1t", "b0o", "b0t", "c1t", "c1o", "c0t", "c0o")
+SPREAD, AHEAD, BEHIND, FAR_K, FAR_V, RELAY = range(6)
+
 BASE = {"b": 0, "c": 4, "d": 6}
+FIRST = ("b0", "c0", "c1", "b1", "b2", "d0")
+LATE = ("b3", "d1")
+SECOND = ("d1", "d0", "b3", "b2", "c1", "b1", "b0", "c0")
 
 
 def code(name):
-    return (BASE[name[0]] + int(name[1])) * 2 + (name[2] == "t")
+    return BASE[name[0]] + int(name[1])
+
+
+def pick(step, values):
+    chosen = values[0]
+    for at, value in enumerate(values[1:], 1):
+        chosen = jnp.where(step == at, value, chosen)
+    return chosen
 
 
 def place(letter, n):
     return BASE[letter] + n // 2, n % 2
-
-
-def pick(step, order):
-    chosen = code(order[0])
-    for at, name in enumerate(order[1:], 1):
-        chosen = jnp.where(step == at, code(name), chosen)
-    return chosen // 2, chosen % 2
 
 
 def attend(base, group, count, keys, vals, causal, qs, lives, peak, denom, weighted, peaks, exps, gprobs):
@@ -107,7 +108,7 @@
 def kernel(lengths, q_hbm, pk_hbm, pv_hbm, rk_hbm, rv_hbm, g_hbm, dq_hbm, drk_hbm, drv_hbm, dpk_hbm, dpv_hbm,
            q, pk, pv, rk, rv, g, dq_out, drk, drv, dpk, dpv,
            qs, lives, peak, denom, weighted, peaks, exps, gprobs, dq, dq_send, dq_in,
-           stat_out, stat_in, packed, kv, own, half_out, half_in, ring_out, ring_in, z_out, z_in,
+           stat_out, stat_in, packed, passing, returning, kv, own, half_out, half_in, ring_out, ring_in, z_out, z_in,
            local_s, swap_s, swap_r, stat_s, stat_r, dq_s, dq_r, get_s, get_r, half_s, half_r, ring_s, ring_r, z_s, z_r):
     heads = q.shape[1] // HD
     resp, tensor = lax.axis_index("resp"), lax.axis_index("tensor")
@@ -123,7 +124,7 @@
         return pl.ds(pl.multiple_of(index * HD, HD), HD)
 
     barrier = pltpu.get_barrier_semaphore()
-    for other in (up, down, twin, along(1), along(2), along(3)):
+    for other in (up, down, twin, along(1), along(3)):
         pl.semaphore_signal(barrier, inc=1, device_id=other, device_id_type=MESH)
     moves_in = [
         pltpu.make_async_copy(src, dst, local_s.at[i])
@@ -142,7 +143,11 @@
 
     def get(n, kind):
         mine, far = kv.at[*place("c", n)], kv.at[*place("d", n)]
-        if kind == SPREAD:
+        if kind == RELAY:
+            ends = [(packed.at[n, part], passing.at[part], along((1, 3)[part])) for part in range(2)]
+        elif kind == SPREAD and n == 3:
+            ends = [(passing.at[part], mine.at[part], along((1, 3)[part])) for part in range(2)]
+        elif kind == SPREAD:
             ends = [(packed.at[n, part], mine.at[part], along(TURN[n])) for part in range(2)]
         elif kind == AHEAD:
             ends = [(mine.at[part], kv.at[n, 0, part], up) for part in range(2)]
@@ -174,6 +179,11 @@
         received(get(n, BEHIND))
         start(get(n, FAR_V))
 
+    def relay_out():
+        for first_hop, second_hop in zip(get(3, RELAY), get(3, SPREAD)):
+            first_hop.wait_recv()
+            second_hop.start()
+
     def swap():
         return [
             send(ref.at[h], ref.at[heads + h], (swap_s, swap_r), (i, h), twin)
@@ -191,10 +201,11 @@
         cols = columns((tensor + TURN[n]) % 4)
         packed[n, 0] = pk[:, cols]
         packed[n, 1] = pv[:, cols]
-    pl.semaphore_wait(barrier, 6)
+    pl.semaphore_wait(barrier, 5)
     begin(0)
-    for n in range(1, ROUNDS):
-        start(get(n, SPREAD))
+    start(get(1, SPREAD))
+    start(get(2, SPREAD))
+    start(get(3, RELAY))
     moves_in[2].wait()
     moves_in[3].wait()
     for h in range(heads):
@@ -208,27 +219,24 @@
     denom[...] = jnp.zeros(denom.shape, jnp.float32)
     weighted[...] = jnp.zeros(weighted.shape, jnp.float32)
     dq[...] = jnp.zeros(dq.shape, jnp.float32)
-    own[...] = jnp.zeros(own.shape, jnp.float32)
     causal = lax.broadcasted_iota(jnp.int32, (CHUNK, ROWS), 0) <= lax.broadcasted_iota(jnp.int32, (CHUNK, ROWS), 1)
     sums = (qs, lives, peak, denom, weighted, peaks, exps, gprobs)
-    steps = len(FIRST)
-    attend(steps * heads, 0, heads, rk[...], rv[...], causal, *sums)
+    steps = len(SECOND)
+    attend(2 * steps * heads, 0, heads, rk[...], rv[...], causal, *sums)
 
     def far_received(*rounds):
         for n in rounds:
             received(get(n, FAR_K) + get(n, FAR_V))
 
     before = {
-        "b0o": (lambda: forward(0),),
-        "b0t": (lambda: received(swap()),),
-        "d0t": (lambda: far_received(0, 1),),
-        "d1t": (lambda: far_received(2, 3),),
+        "b0": (lambda: forward(0), lambda: received(swap())),
+        "d0": (lambda: far_received(0, 1),),
     }
     after = {
-        "b0o": (lambda: begin(1), lambda: begin(2)),
-        "c0t": (lambda: begin(3),),
-        "c1t": (lambda: forward(1), lambda: forward(2)),
-        "b2t": (lambda: forward(3),),
+        "b0": (lambda: begin(1), lambda: begin(2), relay_out),
+        "c0": (lambda: begin(3),),
+        "c1": (lambda: forward(1), lambda: forward(2)),
+        "b2": (lambda: forward(3),),
     }
 
     def serve(step, order, table):
@@ -238,29 +246,42 @@
                 for job in jobs:
                     job()
 
-    def first(step, carry):
-        chunk, half = pick(step, FIRST)
-        serve(step, FIRST, before)
+    def tell(half):
+        return send(stat_out.at[half], stat_in.at[1 - half], (stat_s, stat_r), 1 - half, twin)
+
+    def take(chunk, half):
         keys = kv[chunk, :, 0].reshape(CHUNK, HD)
         vals = kv[chunk, :, 1].reshape(CHUNK, HD)
         attend((chunk * 2 + half) * heads, half * heads, heads, keys, vals, None, *sums)
+
+    def first(step, carry):
+        chunk = pick(step, [code(name) for name in FIRST])
+        serve(step, FIRST, before)
+        take(chunk, 0)
+        take(chunk, 1)
         serve(step, FIRST, after)
-
-        @pl.when(step == FIRST.index("d1t"))
-        def _():
-            join_sums(heads, heads, peak, denom, weighted, stat_out.at[1])
-            tell(1).start()
-
         return carry
 
-    def tell(half):
-        return send(stat_out.at[half], stat_in.at[1 - half], (stat_s, stat_r), 1 - half, twin)
-
-    lax.fori_loop(0, steps, first, 0)
+    lax.fori_loop(0, len(FIRST), first, 0)
+    far_received(2, 3)
+    for name in LATE:
+        take(code(name), 1)
+    join_sums(heads, heads, peak, denom, weighted, stat_out.at[1])
+    tell(1).start()
+    for name in LATE:
+        take(code(name), 0)
     join_sums(0, heads, peak, denom, weighted, stat_out.at[0])
     tell(0).start()
+    for n in range(ROUNDS):
+        for kind in range(SPREAD if n else AHEAD, FAR_V + 1):
+            for copy in get(n, kind):
+                copy.wait_send()
+    for copy in get(3, RELAY) + swap():
+        copy.wait_send()
     tell(1).wait_recv()
     finish_stats(0, heads, stat_out.at[0], stat_in.at[0], peak, weighted)
+    tell(0).wait_recv()
+    finish_stats(heads, heads, stat_out.at[1], stat_in.at[1], peak, weighted)
 
     def to_half(n, part):
         return send(half_out.at[n, part], half_in.at[n, part], (half_s, half_r), (n, part), (up, down)[part])
@@ -272,9 +293,21 @@
         ]
 
     def to_holder(n):
+        if n == 3:
+            ends = [(returning.at[part], along((1, 3)[part])) for part in range(2)]
+        else:
+            ends = [(z_out.at[n, part], along(4 - TURN[n])) for part in range(2)]
+        return [send(src, z_in.at[n, part], (z_s, z_r), (n, part), to) for part, (src, to) in enumerate(ends)]
+
+    def to_relay():
         return [
-            send(z_out.at[n, part], z_in.at[n, part], (z_s, z_r), (n, part), along(4 - TURN[n])) for part in range(2)
+            send(z_out.at[3, part], returning.at[part], (z_s, z_r), (0, part), along((1, 3)[part])) for part in range(2)
         ]
+
+    def relay_back():
+        for first_hop, second_hop in zip(to_relay(), to_holder(3)):
+            first_hop.wait_recv()
+            second_hop.start()
 
     def to_owner(h):
         return send(dq_send.at[h], dq_in.at[h], (dq_s, dq_r), h, twin)
@@ -301,11 +334,7 @@
 
     def hand_over(n):
         z_out[n] = total(n).astype(jnp.bfloat16)
-        start(to_holder(n))
-
-    def learn():
-        tell(0).wait_recv()
-        finish_stats(heads, heads, stat_out.at[1], stat_in.at[1], peak, weighted)
+        start(to_relay() if n == 3 else to_holder(n))
 
     def return_queries():
         for h in range(heads):
@@ -313,32 +342,27 @@
             to_owner(h).start()
 
     services = {
-        "d0o": (learn,),
-        "d1t": (lambda: halves(3), lambda: halves(2)),
-        "d0t": (lambda: halves(1), lambda: halves(0)),
-        "b2t": (lambda: relay(3), lambda: relay(2)),
-        "b1t": (lambda: relay(1),),
-        "b0t": (lambda: relay(0),),
-        "c1o": (lambda: hand_over(3), lambda: hand_over(2)),
-        "c0t": (return_queries,),
-        "c0o": (lambda: hand_over(1),),
+        "d1": (lambda: halves(3), lambda: halves(2)),
+        "d0": (lambda: halves(1), lambda: halves(0)),
+        "b2": (lambda: relay(3), lambda: relay(2)),
+        "b1": (lambda: relay(1), lambda: hand_over(3)),
+        "b0": (lambda: relay(0), lambda: hand_over(2)),
+        "c0": (return_queries, relay_back, lambda: hand_over(1)),
     }
 
     def second(step, carry):
-        chunk, half = pick(step, SECOND)
+        chunk = pick(step, [code(name) for name in SECOND])
         keys = kv[chunk, :, 0].reshape(CHUNK, HD)
         grad_k, grad_v = grads(
-            (chunk * 2 + half) * heads, half * heads, heads, keys, qs, lives, peak, weighted, peaks, exps, gprobs, dq
+            chunk * 2 * heads, 0, 2 * heads, keys, qs, lives, peak, weighted, peaks, exps, gprobs, dq
         )
-        grad_k = (grad_k * SCALE).reshape(2, QUARTER, HD)
-        grad_v = grad_v.reshape(2, QUARTER, HD)
-        own[chunk, :, 0] += grad_k
-        own[chunk, :, 1] += grad_v
+        own[chunk, :, 0] = (grad_k * SCALE).reshape(2, QUARTER, HD)
+        own[chunk, :, 1] = grad_v.reshape(2, QUARTER, HD)
         serve(step, SECOND, services)
         return carry
 
     lax.fori_loop(0, steps, second, 0)
-    grad_k, grad_v = grads(steps * heads, 0, heads, rk[...], qs, lives, peak, weighted, peaks, exps, gprobs, dq)
+    grad_k, grad_v = grads(2 * steps * heads, 0, heads, rk[...], qs, lives, peak, weighted, peaks, exps, gprobs, dq)
     drk[...] = grad_k * SCALE
     drv[...] = grad_v
     moves_out = [
@@ -363,10 +387,8 @@
         dpv[:, cols] = wide(z_in[n, 1])
     moves_out[3].start()
     moves_out[4].start()
-    sent = swap() + [tell(0), tell(1)] + [to_owner(h) for h in range(heads)]
+    sent = to_relay() + [tell(0), tell(1)] + [to_owner(h) for h in range(heads)]
     for n in range(ROUNDS):
-        for kind in range(SPREAD if n else AHEAD, FAR_V + 1):
-            sent += get(n, kind)
         sent += [to_half(n, 0), to_half(n, 1)] + to_ring(n, 0) + to_ring(n, 1)
         if n:
             sent += to_holder(n)
@@ -393,7 +415,7 @@
 
 def local(prompt_k, prompt_v, resp_q, resp_k, resp_v, resp_grad, lengths):
     heads = resp_q.shape[1] // HD
-    blocks = (len(FIRST) + 1) * heads
+    blocks = (2 * len(SECOND) + 1) * heads
     anywhere = pl.BlockSpec(memory_space=pl.ANY)
     f32, bf16 = jnp.float32, jnp.bfloat16
     stat = pltpu.VMEM((2 * heads, 8, ROWS), f32)
@@ -426,6 +448,8 @@
             pltpu.VMEM((2, 3, 8, ROWS), f32),
             pltpu.VMEM((2, 3, 8, ROWS), f32),
             pltpu.VMEM((ROUNDS,) + piece, bf16),
+            pltpu.VMEM(piece, bf16),
+            pltpu.VMEM(piece, bf16),
             pltpu.VMEM((2 * ROUNDS, 2) + piece, bf16),
             pltpu.VMEM((2 * ROUNDS, 2) + piece, f32),
             pltpu.VMEM((ROUNDS,) + piece, bf16),
@@ -438,7 +462,7 @@
             *sems(2, heads),
             *sems(2),
             *sems(heads),
-            *sems(ROUNDS, 5, 2),
+            *sems(ROUNDS, 6, 2),
             *sems(ROUNDS, 2),
             *sems(ROUNDS, 2, 2),
             *sems(ROUNDS, 2),

time: 54.4 us -> 54.9 us (level)
  no operation moved by 1% of the time
where the time goes in v3:
time: 54.9 us; the launch traced here: 54.3 us
  Pallas kernels  53 us (97%)
  between operations  1.29 us (2%)
    pallas_call x1, Pallas kernels, local(): pl.pallas_call(kernel, out_shape=outs, in_specs=[pl.BlockSpec(memory_spac...  50.7 us
    pallas_call x1, Pallas kernels, local(): pl.pallas_call(copy_kernel, out_shape=outs, in_specs=[anywhere] * 5, out_...  2.27 us

profile of v3, /device:TPU:1, one launch (start us, length us, event | category | flops | bytes accessed | tf_op | source)
XLA Modules:
  0.0 54.3 jit_solution(15784690753255970131)
XLA Ops:
  1.3 50.7 %shard_map.110 = (f32[256,640]{1,0:T(8,128)}, f32[256,128]{1,0:T(8,128)}, f32[256,128]{1,0:T(8,128)}, f32[128,512]{1,0:T(8,128)}, f32[128,512]{1,0:T(8,128)}) custom-call(s32[1]{0:T(128)S(6)} %copy.12.lengths, bf16[256,640]{1,0:T(8,128)(2,1)} %q_hbm.1, bf16[128,512]{1,0:T(8,128)(2,1)} %pk_hbm.1, bf16[128,512]{1,0:T(8,128)(2,1)} %pv_hbm.1, ...), custom_call_target="tpu_custom_call" | custom-call | flops 7130316800 | bytes 3145728 | tf_op jit(solution)/shard_map/pallas_call | solution.py:429
  52.0 2.3 %shard_map.111 = (f32[256,640]{1,0:T(8,128)}, f32[256,128]{1,0:T(8,128)}, f32[256,128]{1,0:T(8,128)}, f32[128,512]{1,0:T(8,128)}, f32[128,512]{1,0:T(8,128)}) custom-call(f32[256,640]{1,0:T(8,128)} %get-tuple-element.10.refs_0_, f32[256,128]{1,0:T(8,128)} %get-tuple-element.11.refs_1_, f32[256,128]{1,0:T(8,128)} %get-tuple-element.12.refs_2_, ...), custom_call_target="tpu_custom_call" | custom-call | tf_op jit(solution)/shard_map/pallas_call | solution.py:475

commit v4 on v3

--- a/solution.py
+++ b/solution.py
@@ -27,7 +27,7 @@
 SPREAD, AHEAD, BEHIND, FAR_K, FAR_V, RELAY = range(6)
 
 BASE = {"b": 0, "c": 4, "d": 6}
-FIRST = ("b0", "c0", "c1", "b1", "b2", "d0")
+FIRST = (("b0o", "c0o"), ("b0t", "c0t"), ("c1o", "c1t"), ("b1o", "b1t"), ("b2o", "b2t"), ("d0o", "d0t"))
 LATE = ("b3", "d1")
 SECOND = ("d1", "d0", "b3", "b2", "c1", "b1", "b0", "c0")
 
@@ -148,11 +148,11 @@
         elif kind == SPREAD and n == 3:
             ends = [(passing.at[part], mine.at[part], along((1, 3)[part])) for part in range(2)]
         elif kind == SPREAD:
-            ends = [(packed.at[n, part], mine.at[part], along(TURN[n])) for part in range(2)]
+            ends = [(packed.at[n], mine, along(TURN[n]))]
         elif kind == AHEAD:
-            ends = [(mine.at[part], kv.at[n, 0, part], up) for part in range(2)]
+            ends = [(mine, kv.at[n, 0], up)]
         elif kind == BEHIND:
-            ends = [(mine.at[part], kv.at[n, 1, part], down) for part in range(2)]
+            ends = [(mine, kv.at[n, 1], down)]
         elif kind == FAR_K:
             ends = [(kv.at[n, 0, 0], far.at[0], up)]
         else:
@@ -185,11 +185,8 @@
             second_hop.start()
 
     def swap():
-        return [
-            send(ref.at[h], ref.at[heads + h], (swap_s, swap_r), (i, h), twin)
-            for h in range(heads)
-            for i, ref in enumerate((qs, lives))
-        ]
+        here, there = pl.ds(0, heads), pl.ds(heads, heads)
+        return [send(ref.at[here], ref.at[there], (swap_s, swap_r), i, twin) for i, ref in enumerate((qs, lives))]
 
     positions = lax.broadcasted_iota(jnp.int32, (ROWS, HD), 0)
     alive = positions < lengths[0]
@@ -229,14 +226,15 @@
             received(get(n, FAR_K) + get(n, FAR_V))
 
     before = {
-        "b0": (lambda: forward(0), lambda: received(swap())),
-        "d0": (lambda: far_received(0, 1),),
+        "b0o": (lambda: forward(0), lambda: begin(1), lambda: begin(2)),
+        "b0t": (lambda: received(swap()),),
+        "d0o": (lambda: far_received(0, 1),),
     }
     after = {
-        "b0": (lambda: begin(1), lambda: begin(2), relay_out),
-        "c0": (lambda: begin(3),),
-        "c1": (lambda: forward(1), lambda: forward(2)),
-        "b2": (lambda: forward(3),),
+        "b0o": (relay_out,),
+        "b0t": (lambda: begin(3),),
+        "c1o": (lambda: forward(1), lambda: forward(2)),
+        "b2o": (lambda: forward(3),),
     }
 
     def serve(step, order, table):
@@ -255,11 +253,11 @@
         attend((chunk * 2 + half) * heads, half * heads, heads, keys, vals, None, *sums)
 
     def first(step, carry):
-        chunk = pick(step, [code(name) for name in FIRST])
-        serve(step, FIRST, before)
-        take(chunk, 0)
-        take(chunk, 1)
-        serve(step, FIRST, after)
+        leads = [pair[0] for pair in FIRST]
+        serve(step, leads, before)
+        for at in range(2):
+            take(pick(step, [code(pair[at]) for pair in FIRST]), pick(step, [int(pair[at][2] == "t") for pair in FIRST]))
+        serve(step, leads, after)
         return carry
 
     lax.fori_loop(0, len(FIRST), first, 0)
@@ -287,16 +285,13 @@
         return send(half_out.at[n, part], half_in.at[n, part], (half_s, half_r), (n, part), (up, down)[part])
 
     def to_ring(n, way):
-        return [
-            send(ring_out.at[n, way, part], ring_in.at[n, way, part], (ring_s, ring_r), (n, way, part), (up, down)[way])
-            for part in range(2)
-        ]
+        return send(ring_out.at[n, way], ring_in.at[n, way], (ring_s, ring_r), (n, way), (up, down)[way])
 
     def to_holder(n):
         if n == 3:
             ends = [(returning.at[part], along((1, 3)[part])) for part in range(2)]
         else:
-            ends = [(z_out.at[n, part], along(4 - TURN[n])) for part in range(2)]
+            return [send(z_out.at[n], z_in.at[n], (z_s, z_r), (n, 0), along(4 - TURN[n]))]
         return [send(src, z_in.at[n, part], (z_s, z_r), (n, part), to) for part, (src, to) in enumerate(ends)]
 
     def to_relay():
@@ -309,8 +304,8 @@
             first_hop.wait_recv()
             second_hop.start()
 
-    def to_owner(h):
-        return send(dq_send.at[h], dq_in.at[h], (dq_s, dq_r), h, twin)
+    def to_owner():
+        return send(dq_send, dq_in, (dq_s, dq_r), 0, twin)
 
     def wide(ref):
         return ref.astype(jnp.float32)
@@ -326,10 +321,10 @@
             part = own[n, 1 - way]
             ring_out[n, way, way] = (part[way] + wide(half_in[n, way])).astype(jnp.bfloat16)
             ring_out[n, way, 1 - way] = part[1 - way].astype(jnp.bfloat16)
-            start(to_ring(n, way))
+            to_ring(n, way).start()
 
     def total(n):
-        received(to_ring(n, 0) + to_ring(n, 1))
+        received([to_ring(n, 0), to_ring(n, 1)])
         return own[place("c", n)] + wide(ring_in[n, 0]) + wide(ring_in[n, 1])
 
     def hand_over(n):
@@ -339,7 +334,7 @@
     def return_queries():
         for h in range(heads):
             dq_send[h] = dq[heads + h].astype(jnp.bfloat16)
-            to_owner(h).start()
+        to_owner().start()
 
     services = {
         "d1": (lambda: halves(3), lambda: halves(2)),
@@ -373,8 +368,8 @@
     ]
     moves_out[0].start()
     moves_out[1].start()
+    to_owner().wait_recv()
     for h in range(heads):
-        to_owner(h).wait_recv()
         dq_out[:, h * HD : (h + 1) * HD] = (dq[h] + wide(dq_in[h])).T * SCALE
     moves_out[2].start()
     sums_now = total(0)
@@ -387,9 +382,9 @@
         dpv[:, cols] = wide(z_in[n, 1])
     moves_out[3].start()
     moves_out[4].start()
-    sent = to_relay() + [tell(0), tell(1)] + [to_owner(h) for h in range(heads)]
+    sent = to_relay() + [tell(0), tell(1), to_owner()]
     for n in range(ROUNDS):
-        sent += [to_half(n, 0), to_half(n, 1)] + to_ring(n, 0) + to_ring(n, 1)
+        sent += [to_half(n, 0), to_half(n, 1), to_ring(n, 0), to_ring(n, 1)]
         if n:
             sent += to_holder(n)
     for copy in sent:
@@ -459,12 +454,12 @@
             pltpu.VMEM((ROUNDS,) + piece, bf16),
             pltpu.VMEM((ROUNDS,) + piece, bf16),
             pltpu.SemaphoreType.DMA((11,)),
-            *sems(2, heads),
             *sems(2),
-            *sems(heads),
+            *sems(2),
+            *sems(1),
             *sems(ROUNDS, 6, 2),
             *sems(ROUNDS, 2),
-            *sems(ROUNDS, 2, 2),
+            *sems(ROUNDS, 2),
             *sems(ROUNDS, 2),
         ],
         compiler_params=pltpu.CompilerParams(

time: 54.9 us -> 55.9 us (1.018)
  Pallas kernels: 53 us -> 54.5 us
    pallas_call x1, Pallas kernels: 50.7 us -> 52.2 us  [local(): pl.pallas_call(kernel, out_shape=outs, in_specs=[pl.BlockSpec(memory_spac...]
where the time goes in v4:
time: 55.9 us; the launch traced here: 55.8 us
  Pallas kernels  54.5 us (97%)
  between operations  1.29 us (2%)
    pallas_call x1, Pallas kernels, local(): pl.pallas_call(kernel, out_shape=outs, in_specs=[pl.BlockSpec(memory_spac...  52.2 us
    pallas_call x1, Pallas kernels, local(): pl.pallas_call(copy_kernel, out_shape=outs, in_specs=[anywhere] * 5, out_...  2.27 us

profile of v4, /device:TPU:1, one launch (start us, length us, event | category | flops | bytes accessed | tf_op | source)
XLA Modules:
  0.0 55.8 jit_solution(4664710209978132498)
XLA Ops:
  1.3 52.2 %shard_map.110 = (f32[256,640]{1,0:T(8,128)}, f32[256,128]{1,0:T(8,128)}, f32[256,128]{1,0:T(8,128)}, f32[128,512]{1,0:T(8,128)}, f32[128,512]{1,0:T(8,128)}) custom-call(s32[1]{0:T(128)S(6)} %copy.12.lengths, bf16[256,640]{1,0:T(8,128)(2,1)} %q_hbm.1, bf16[128,512]{1,0:T(8,128)(2,1)} %pk_hbm.1, bf16[128,512]{1,0:T(8,128)(2,1)} %pv_hbm.1, ...), custom_call_target="tpu_custom_call" | custom-call | flops 7130316800 | bytes 3145728 | tf_op jit(solution)/shard_map/pallas_call | solution.py:424
  53.5 2.3 %shard_map.111 = (f32[256,640]{1,0:T(8,128)}, f32[256,128]{1,0:T(8,128)}, f32[256,128]{1,0:T(8,128)}, f32[128,512]{1,0:T(8,128)}, f32[128,512]{1,0:T(8,128)}) custom-call(f32[256,640]{1,0:T(8,128)} %get-tuple-element.10.refs_0_, f32[256,128]{1,0:T(8,128)} %get-tuple-element.11.refs_1_, f32[256,128]{1,0:T(8,128)} %get-tuple-element.12.refs_2_, ...), custom_call_target="tpu_custom_call" | custom-call | tf_op jit(solution)/shard_map/pallas_call | solution.py:470

commit v5 on v4

--- a/solution.py
+++ b/solution.py
@@ -26,14 +26,15 @@
 TURN = (0, 1, 3, 2)
 SPREAD, AHEAD, BEHIND, FAR_K, FAR_V, RELAY = range(6)
 
-BASE = {"b": 0, "c": 4, "d": 6}
-FIRST = (("b0o", "c0o"), ("b0t", "c0t"), ("c1o", "c1t"), ("b1o", "b1t"), ("b2o", "b2t"), ("d0o", "d0t"))
-LATE = ("b3", "d1")
-SECOND = ("d1", "d0", "b3", "b2", "c1", "b1", "b0", "c0")
-
-
-def code(name):
-    return BASE[name[0]] + int(name[1])
+CHUNKS = ("b0", "b1", "b2", "b3", "e0", "m", "f", "e3")
+FIRST = ("b0", "e0", "m", "b1", "b2", "f")
+SECOND = ("e3", "f", "b3", "b2", "b1", "m", "e0", "b0")
+OWN = (("e0", 0), ("m", 0), ("m", 1), ("e3", 0))
+FAR = (("e0", 1), ("f", 0), ("f", 1), ("e3", 1))
+
+
+def place(where, n):
+    return CHUNKS.index(where[n][0]), where[n][1]
 
 
 def pick(step, values):
@@ -41,10 +42,6 @@
     for at, value in enumerate(values[1:], 1):
         chosen = jnp.where(step == at, value, chosen)
     return chosen
-
-
-def place(letter, n):
-    return BASE[letter] + n // 2, n % 2
 
 
 def attend(base, group, count, keys, vals, causal, qs, lives, peak, denom, weighted, peaks, exps, gprobs):
@@ -142,7 +139,7 @@
         )
 
     def get(n, kind):
-        mine, far = kv.at[*place("c", n)], kv.at[*place("d", n)]
+        mine, far = kv.at[*place(OWN, n)], kv.at[*place(FAR, n)]
         if kind == RELAY:
             ends = [(packed.at[n, part], passing.at[part], along((1, 3)[part])) for part in range(2)]
         elif kind == SPREAD and n == 3:
@@ -226,15 +223,12 @@
             received(get(n, FAR_K) + get(n, FAR_V))
 
     before = {
-        "b0o": (lambda: forward(0), lambda: begin(1), lambda: begin(2)),
-        "b0t": (lambda: received(swap()),),
-        "d0o": (lambda: far_received(0, 1),),
-    }
-    after = {
-        "b0o": (relay_out,),
-        "b0t": (lambda: begin(3),),
-        "c1o": (lambda: forward(1), lambda: forward(2)),
-        "b2o": (lambda: forward(3),),
+        "b0": (lambda: forward(0), lambda: received(swap())),
+        "e0": (lambda: far_received(0),),
+        "m": (relay_out, lambda: begin(1), lambda: begin(2)),
+        "b1": (lambda: forward(1), lambda: forward(2)),
+        "b2": (lambda: begin(3),),
+        "f": (lambda: far_received(1, 2),),
     }
 
     def serve(step, order, table):
@@ -253,21 +247,21 @@
         attend((chunk * 2 + half) * heads, half * heads, heads, keys, vals, None, *sums)
 
     def first(step, carry):
-        leads = [pair[0] for pair in FIRST]
-        serve(step, leads, before)
-        for at in range(2):
-            take(pick(step, [code(pair[at]) for pair in FIRST]), pick(step, [int(pair[at][2] == "t") for pair in FIRST]))
-        serve(step, leads, after)
+        chunk = pick(step, [CHUNKS.index(name) for name in FIRST])
+        serve(step, FIRST, before)
+        take(chunk, 0)
+        take(chunk, 1)
         return carry
 
     lax.fori_loop(0, len(FIRST), first, 0)
-    far_received(2, 3)
-    for name in LATE:
-        take(code(name), 1)
+    forward(3)
+    take(CHUNKS.index("b3"), 1)
+    take(CHUNKS.index("b3"), 0)
+    far_received(3)
+    take(CHUNKS.index("e3"), 1)
     join_sums(heads, heads, peak, denom, weighted, stat_out.at[1])
     tell(1).start()
-    for name in LATE:
-        take(code(name), 0)
+    take(CHUNKS.index("e3"), 0)
     join_sums(0, heads, peak, denom, weighted, stat_out.at[0])
     tell(0).start()
     for n in range(ROUNDS):
@@ -311,7 +305,7 @@
         return ref.astype(jnp.float32)
 
     def halves(n):
-        half_out[n] = own[place("d", n)].astype(jnp.bfloat16)
+        half_out[n] = own[place(FAR, n)].astype(jnp.bfloat16)
         to_half(n, 0).start()
         to_half(n, 1).start()
 
@@ -325,7 +319,7 @@
 
     def total(n):
         received([to_ring(n, 0), to_ring(n, 1)])
-        return own[place("c", n)] + wide(ring_in[n, 0]) + wide(ring_in[n, 1])
+        return own[place(OWN, n)] + wide(ring_in[n, 0]) + wide(ring_in[n, 1])
 
     def hand_over(n):
         z_out[n] = total(n).astype(jnp.bfloat16)
@@ -337,16 +331,18 @@
         to_owner().start()
 
     services = {
-        "d1": (lambda: halves(3), lambda: halves(2)),
-        "d0": (lambda: halves(1), lambda: halves(0)),
-        "b2": (lambda: relay(3), lambda: relay(2)),
+        "e3": (lambda: halves(3),),
+        "f": (lambda: halves(2), lambda: halves(1)),
+        "b3": (lambda: relay(3),),
+        "b2": (lambda: relay(2),),
         "b1": (lambda: relay(1), lambda: hand_over(3)),
-        "b0": (lambda: relay(0), lambda: hand_over(2)),
-        "c0": (return_queries, relay_back, lambda: hand_over(1)),
+        "m": (lambda: hand_over(2),),
+        "e0": (lambda: halves(0), lambda: hand_over(1)),
+        "b0": (return_queries, relay_back),
     }
 
     def second(step, carry):
-        chunk = pick(step, [code(name) for name in SECOND])
+        chunk = pick(step, [CHUNKS.index(name) for name in SECOND])
         keys = kv[chunk, :, 0].reshape(CHUNK, HD)
         grad_k, grad_v = grads(
             chunk * 2 * heads, 0, 2 * heads, keys, qs, lives, peak, weighted, peaks, exps, gprobs, dq
@@ -360,6 +356,7 @@
     grad_k, grad_v = grads(2 * steps * heads, 0, heads, rk[...], qs, lives, peak, weighted, peaks, exps, gprobs, dq)
     drk[...] = grad_k * SCALE
     drv[...] = grad_v
+    relay(0)
     moves_out = [
         pltpu.make_async_copy(src, dst, local_s.at[6 + i])
         for i, (src, dst) in enumerate((

time: 55.9 us -> 56.1 us (level)
  no operation moved by 1% of the time
where the time goes in v5:
time: 56.1 us; the launch traced here: 56 us
  Pallas kernels  54.7 us (98%)
  between operations  1.29 us (2%)
    pallas_call x1, Pallas kernels, local(): pl.pallas_call(kernel, out_shape=outs, in_specs=[pl.BlockSpec(memory_spac...  52.4 us
    pallas_call x1, Pallas kernels, local(): pl.pallas_call(copy_kernel, out_shape=outs, in_specs=[anywhere] * 5, out_...  2.27 us

profile of v5, /device:TPU:1, one launch (start us, length us, event | category | flops | bytes accessed | tf_op | source)
XLA Modules:
  0.0 56.0 jit_solution(1538784669921477475)
XLA Ops:
  1.3 52.4 %shard_map.110 = (f32[256,640]{1,0:T(8,128)}, f32[256,128]{1,0:T(8,128)}, f32[256,128]{1,0:T(8,128)}, f32[128,512]{1,0:T(8,128)}, f32[128,512]{1,0:T(8,128)}) custom-call(s32[1]{0:T(128)S(6)} %copy.12.lengths, bf16[256,640]{1,0:T(8,128)(2,1)} %q_hbm.1, bf16[128,512]{1,0:T(8,128)(2,1)} %pk_hbm.1, bf16[128,512]{1,0:T(8,128)(2,1)} %pv_hbm.1, ...), custom_call_target="tpu_custom_call" | custom-call | flops 7130316800 | bytes 3145728 | tf_op jit(solution)/shard_map/pallas_call | solution.py:421
  53.7 2.3 %shard_map.111 = (f32[256,640]{1,0:T(8,128)}, f32[256,128]{1,0:T(8,128)}, f32[256,128]{1,0:T(8,128)}, f32[128,512]{1,0:T(8,128)}, f32[128,512]{1,0:T(8,128)}) custom-call(f32[256,640]{1,0:T(8,128)} %get-tuple-element.10.refs_0_, f32[256,128]{1,0:T(8,128)} %get-tuple-element.11.refs_1_, f32[256,128]{1,0:T(8,128)} %get-tuple-element.12.refs_2_, ...), custom_call_target="tpu_custom_call" | custom-call | tf_op jit(solution)/shard_map/pallas_call | solution.py:467

commit v6 on v5

--- a/solution.py
+++ b/solution.py
@@ -145,11 +145,11 @@
         elif kind == SPREAD and n == 3:
             ends = [(passing.at[part], mine.at[part], along((1, 3)[part])) for part in range(2)]
         elif kind == SPREAD:
-            ends = [(packed.at[n], mine, along(TURN[n]))]
+            ends = [(packed.at[n, part], mine.at[part], along(TURN[n])) for part in range(2)]
         elif kind == AHEAD:
-            ends = [(mine, kv.at[n, 0], up)]
+            ends = [(mine.at[part], kv.at[n, 0, part], up) for part in range(2)]
         elif kind == BEHIND:
-            ends = [(mine, kv.at[n, 1], down)]
+            ends = [(mine.at[part], kv.at[n, 1, part], down) for part in range(2)]
         elif kind == FAR_K:
             ends = [(kv.at[n, 0, 0], far.at[0], up)]
         else:
@@ -164,17 +164,19 @@
         for copy in copies:
             copy.wait_recv()
 
-    def begin(n):
+    def begin(n, part):
         if n:
-            received(get(n, SPREAD))
-        start(get(n, AHEAD))
-        start(get(n, BEHIND))
-
-    def forward(n):
-        received(get(n, AHEAD))
-        start(get(n, FAR_K))
-        received(get(n, BEHIND))
-        start(get(n, FAR_V))
+            get(n, SPREAD)[part].wait_recv()
+        get(n, AHEAD)[part].start()
+        get(n, BEHIND)[part].start()
+
+    def forward(n, part):
+        get(n, (AHEAD, BEHIND)[part])[part].wait_recv()
+        start(get(n, (FAR_K, FAR_V)[part]))
+
+    def near_received(n):
+        get(n, AHEAD)[1].wait_recv()
+        get(n, BEHIND)[0].wait_recv()
 
     def relay_out():
         for first_hop, second_hop in zip(get(3, RELAY), get(3, SPREAD)):
@@ -196,9 +198,10 @@
         packed[n, 0] = pk[:, cols]
         packed[n, 1] = pv[:, cols]
     pl.semaphore_wait(barrier, 5)
-    begin(0)
-    start(get(1, SPREAD))
-    start(get(2, SPREAD))
+    for part in range(2):
+        get(1, SPREAD)[part].start()
+        get(2, SPREAD)[part].start()
+        begin(0, part)
     start(get(3, RELAY))
     moves_in[2].wait()
     moves_in[3].wait()
@@ -223,12 +226,15 @@
             received(get(n, FAR_K) + get(n, FAR_V))
 
     before = {
-        "b0": (lambda: forward(0), lambda: received(swap())),
-        "e0": (lambda: far_received(0),),
-        "m": (relay_out, lambda: begin(1), lambda: begin(2)),
-        "b1": (lambda: forward(1), lambda: forward(2)),
-        "b2": (lambda: begin(3),),
-        "f": (lambda: far_received(1, 2),),
+        "b0": (lambda: forward(0, 0), lambda: forward(0, 1), lambda: near_received(0), lambda: received(swap())),
+        "e0": (lambda: begin(1, 0), lambda: begin(2, 0), lambda: far_received(0)),
+        "m": (lambda: begin(1, 1), lambda: begin(2, 1), relay_out),
+        "b1": (
+            lambda: forward(1, 0), lambda: forward(2, 0), lambda: forward(1, 1), lambda: forward(2, 1),
+            lambda: near_received(1),
+        ),
+        "b2": (lambda: near_received(2),),
+        "f": (lambda: begin(3, 0), lambda: begin(3, 1), lambda: far_received(1, 2)),
     }
 
     def serve(step, order, table):
@@ -254,7 +260,9 @@
         return carry
 
     lax.fori_loop(0, len(FIRST), first, 0)
-    forward(3)
+    forward(3, 0)
+    forward(3, 1)
+    near_received(3)
     take(CHUNKS.index("b3"), 1)
     take(CHUNKS.index("b3"), 0)
     far_received(3)
@@ -335,10 +343,9 @@
         "f": (lambda: halves(2), lambda: halves(1)),
         "b3": (lambda: relay(3),),
         "b2": (lambda: relay(2),),
-        "b1": (lambda: relay(1), lambda: hand_over(3)),
-        "m": (lambda: hand_over(2),),
-        "e0": (lambda: halves(0), lambda: hand_over(1)),
-        "b0": (return_queries, relay_back),
+        "b1": (lambda: relay(1),),
+        "e0": (lambda: halves(0), lambda: hand_over(3)),
+        "b0": (return_queries,),
     }
 
     def second(step, carry):
@@ -356,7 +363,7 @@
     grad_k, grad_v = grads(2 * steps * heads, 0, heads, rk[...], qs, lives, peak, weighted, peaks, exps, gprobs, dq)
     drk[...] = grad_k * SCALE
     drv[...] = grad_v
-    relay(0)
+    hand_over(2)
     moves_out = [
         pltpu.make_async_copy(src, dst, local_s.at[6 + i])
         for i, (src, dst) in enumerate((
@@ -369,6 +376,9 @@
     for h in range(heads):
         dq_out[:, h * HD : (h + 1) * HD] = (dq[h] + wide(dq_in[h])).T * SCALE
     moves_out[2].start()
+    hand_over(1)
+    relay_back()
+    relay(0)
     sums_now = total(0)
     dpk[:, columns(tensor)] = sums_now[0]
     dpv[:, columns(tensor)] = sums_now[1]

time: 56.1 us -> 58.1 us (1.036)
  Pallas kernels: 54.7 us -> 56.6 us
    pallas_call x1, Pallas kernels: 52.4 us -> 54.4 us  [local(): pl.pallas_call(kernel, out_shape=outs, in_specs=[pl.BlockSpec(memory_spac...]
where the time goes in v6:
time: 58.1 us; the launch traced here: 57.9 us
  Pallas kernels  56.6 us (97%)
  between operations  1.29 us (2%)
    pallas_call x1, Pallas kernels, local(): pl.pallas_call(kernel, out_shape=outs, in_specs=[pl.BlockSpec(memory_spac...  54.4 us
    pallas_call x1, Pallas kernels, local(): pl.pallas_call(copy_kernel, out_shape=outs, in_specs=[anywhere] * 5, out_...  2.27 us

profile of v6, /device:TPU:1, one launch (start us, length us, event | category | flops | bytes accessed | tf_op | source)
XLA Modules:
  0.0 57.9 jit_solution(1504637601090136020)
XLA Ops:
  1.3 54.4 %shard_map.110 = (f32[256,640]{1,0:T(8,128)}, f32[256,128]{1,0:T(8,128)}, f32[256,128]{1,0:T(8,128)}, f32[128,512]{1,0:T(8,128)}, f32[128,512]{1,0:T(8,128)}) custom-call(s32[1]{0:T(128)S(6)} %copy.12.lengths, bf16[256,640]{1,0:T(8,128)(2,1)} %q_hbm.1, bf16[128,512]{1,0:T(8,128)(2,1)} %pk_hbm.1, bf16[128,512]{1,0:T(8,128)(2,1)} %pv_hbm.1, ...), custom_call_target="tpu_custom_call" | custom-call | flops 7130316800 | bytes 3145728 | tf_op jit(solution)/shard_map/pallas_call | solution.py:431
  55.7 2.3 %shard_map.111 = (f32[256,640]{1,0:T(8,128)}, f32[256,128]{1,0:T(8,128)}, f32[256,128]{1,0:T(8,128)}, f32[128,512]{1,0:T(8,128)}, f32[128,512]{1,0:T(8,128)}) custom-call(f32[256,640]{1,0:T(8,128)} %get-tuple-element.10.refs_0_, f32[256,128]{1,0:T(8,128)} %get-tuple-element.11.refs_1_, f32[256,128]{1,0:T(8,128)} %get-tuple-element.12.refs_2_, ...), custom_call_target="tpu_custom_call" | custom-call | tf_op jit(solution)/shard_map/pallas_call | solution.py:477

commit v7 on v2

--- a/solution.py
+++ b/solution.py
@@ -27,7 +27,7 @@
 SPREAD, AHEAD, BEHIND, FAR_K, FAR_V = range(5)
 
 FIRST = ("b0o", "b0t", "c0o", "c0t", "c1o", "c1t", "b1o", "b1t", "b2o", "b2t", "b3t", "d0t", "b3o", "d1t", "d0o", "d1o")
-SECOND = ("d1o", "d0o", "d1t", "d0t", "b3o", "b3t", "b2o", "b2t", "b1o", "b1t", "b0o", "b0t", "c1t", "c1o", "c0t", "c0o")
+SECOND = ("d1o", "d0o", "d1t", "d0t", "b3o", "b3t", "b2o", "b2t", "b1o", "b1t", "c1t", "c1o", "c0t", "c0o", "b0t", "b0o")
 BASE = {"b": 0, "c": 4, "d": 6}
 
 
@@ -227,8 +227,8 @@
     after = {
         "b0o": (lambda: begin(1), lambda: begin(2)),
         "c0t": (lambda: begin(3),),
-        "c1t": (lambda: forward(1), lambda: forward(2)),
-        "b2t": (lambda: forward(3),),
+        "c1o": (lambda: forward(1), lambda: forward(2)),
+        "b2o": (lambda: forward(3),),
     }
 
     def serve(step, order, table):
@@ -318,10 +318,10 @@
         "d0t": (lambda: halves(1), lambda: halves(0)),
         "b2t": (lambda: relay(3), lambda: relay(2)),
         "b1t": (lambda: relay(1),),
-        "b0t": (lambda: relay(0),),
         "c1o": (lambda: hand_over(3), lambda: hand_over(2)),
-        "c0t": (return_queries,),
         "c0o": (lambda: hand_over(1),),
+        "b0t": (return_queries,),
+        "b0o": (lambda: relay(0),),
     }
 
     def second(step, carry):

time: 54.4 us -> 54.3 us (level)
  the two profiles are of different devices: /device:TPU:1 before, /device:TPU:8 now
where the time goes in v7:
time: 54.3 us; the launch traced here: 54.1 us
  Pallas kernels  52.9 us (97%)
  between operations  1.29 us (2%)
    pallas_call x1, Pallas kernels, local(): pl.pallas_call(kernel, out_shape=outs, in_specs=[pl.BlockSpec(memory_spac...  50.6 us
    pallas_call x1, Pallas kernels, local(): pl.pallas_call(copy_kernel, out_shape=outs, in_specs=[anywhere] * 5, out_...  2.27 us

profile of v7, /device:TPU:8, one launch (start us, length us, event | category | flops | bytes accessed | tf_op | source)
XLA Modules:
  0.0 54.1 jit_solution(11449253717632686572)
XLA Ops:
  1.3 50.6 %shard_map.110 = (f32[256,640]{1,0:T(8,128)}, f32[256,128]{1,0:T(8,128)}, f32[256,128]{1,0:T(8,128)}, f32[128,512]{1,0:T(8,128)}, f32[128,512]{1,0:T(8,128)}) custom-call(s32[1]{0:T(128)S(6)} %copy.12.lengths, bf16[256,640]{1,0:T(8,128)(2,1)} %q_hbm.1, bf16[128,512]{1,0:T(8,128)(2,1)} %pk_hbm.1, bf16[128,512]{1,0:T(8,128)(2,1)} %pv_hbm.1, ...), custom_call_target="tpu_custom_call" | custom-call | flops 7130316800 | bytes 3145728 | tf_op jit(solution)/shard_map/pallas_call | solution.py:407
  51.9 2.3 %shard_map.111 = (f32[256,640]{1,0:T(8,128)}, f32[256,128]{1,0:T(8,128)}, f32[256,128]{1,0:T(8,128)}, f32[128,512]{1,0:T(8,128)}, f32[128,512]{1,0:T(8,128)}) custom-call(f32[256,640]{1,0:T(8,128)} %get-tuple-element.10.refs_0_, f32[256,128]{1,0:T(8,128)} %get-tuple-element.11.refs_1_, f32[256,128]{1,0:T(8,128)} %get-tuple-element.12.refs_2_, ...), custom_call_target="tpu_custom_call" | custom-call | tf_op jit(solution)/shard_map/pallas_call | solution.py:451

commit v8 on v7

--- a/solution.py
+++ b/solution.py
@@ -26,7 +26,7 @@
 TURN = (0, 1, 3, 2)
 SPREAD, AHEAD, BEHIND, FAR_K, FAR_V = range(5)
 
-FIRST = ("b0o", "b0t", "c0o", "c0t", "c1o", "c1t", "b1o", "b1t", "b2o", "b2t", "b3t", "d0t", "b3o", "d1t", "d0o", "d1o")
+FIRST = ("b0o", "b0t", "c0o", "c0t", "b1o", "b1t", "b2o", "b2t", "d0o", "d0t", "c1o", "c1t", "b3t", "b3o", "d1t", "d1o")
 SECOND = ("d1o", "d0o", "d1t", "d0t", "b3o", "b3t", "b2o", "b2t", "b1o", "b1t", "c1t", "c1o", "c0t", "c0o", "b0t", "b0o")
 BASE = {"b": 0, "c": 4, "d": 6}
 
@@ -221,14 +221,15 @@
     before = {
         "b0o": (lambda: forward(0),),
         "b0t": (lambda: received(swap()),),
-        "d0t": (lambda: far_received(0, 1),),
+        "b1o": (lambda: forward(1),),
+        "b2o": (lambda: forward(2),),
+        "d0o": (lambda: far_received(0, 1),),
+        "b3t": (lambda: forward(3),),
         "d1t": (lambda: far_received(2, 3),),
     }
     after = {
         "b0o": (lambda: begin(1), lambda: begin(2)),
-        "c0t": (lambda: begin(3),),
-        "c1o": (lambda: forward(1), lambda: forward(2)),
-        "b2o": (lambda: forward(3),),
+        "b2t": (lambda: begin(3),),
     }
 
     def serve(step, order, table):

time: 54.3 us -> 56.7 us (1.044)
  the two profiles are of different devices: /device:TPU:8 before, /device:TPU:1 now
where the time goes in v8:
time: 56.7 us; the launch traced here: 56.6 us
  Pallas kernels  55.3 us (98%)
  between operations  1.29 us (2%)
    pallas_call x1, Pallas kernels, local(): pl.pallas_call(kernel, out_shape=outs, in_specs=[pl.BlockSpec(memory_spac...  53 us
    pallas_call x1, Pallas kernels, local(): pl.pallas_call(copy_kernel, out_shape=outs, in_specs=[anywhere] * 5, out_...  2.27 us

profile of v8, /device:TPU:1, one launch (start us, length us, event | category | flops | bytes accessed | tf_op | source)
XLA Modules:
  0.0 56.6 jit_solution(7231516923113420898)
XLA Ops:
  1.3 53.0 %shard_map.110 = (f32[256,640]{1,0:T(8,128)}, f32[256,128]{1,0:T(8,128)}, f32[256,128]{1,0:T(8,128)}, f32[128,512]{1,0:T(8,128)}, f32[128,512]{1,0:T(8,128)}) custom-call(s32[1]{0:T(128)S(6)} %copy.12.lengths, bf16[256,640]{1,0:T(8,128)(2,1)} %q_hbm.1, bf16[128,512]{1,0:T(8,128)(2,1)} %pk_hbm.1, bf16[128,512]{1,0:T(8,128)(2,1)} %pv_hbm.1, ...), custom_call_target="tpu_custom_call" | custom-call | flops 7130316800 | bytes 3145728 | tf_op jit(solution)/shard_map/pallas_call | solution.py:408
  54.3 2.3 %shard_map.111 = (f32[256,640]{1,0:T(8,128)}, f32[256,128]{1,0:T(8,128)}, f32[256,128]{1,0:T(8,128)}, f32[128,512]{1,0:T(8,128)}, f32[128,512]{1,0:T(8,128)}) custom-call(f32[256,640]{1,0:T(8,128)} %get-tuple-element.10.refs_0_, f32[256,128]{1,0:T(8,128)} %get-tuple-element.11.refs_1_, f32[256,128]{1,0:T(8,128)} %get-tuple-element.12.refs_2_, ...), custom_call_target="tpu_custom_call" | custom-call | tf_op jit(solution)/shard_map/pallas_call | solution.py:452

commit v9 on v7

--- a/solution.py
+++ b/solution.py
@@ -24,9 +24,9 @@
 QUARTER = 128
 ROUNDS = 4
 TURN = (0, 1, 3, 2)
-SPREAD, AHEAD, BEHIND, FAR_K, FAR_V = range(5)
-
-FIRST = ("b0o", "b0t", "c0o", "c0t", "c1o", "c1t", "b1o", "b1t", "b2o", "b2t", "b3t", "d0t", "b3o", "d1t", "d0o", "d1o")
+SPREAD, AHEAD, BEHIND, ACROSS = range(4)
+
+FIRST = ("b0o", "c0o", "b0t", "c0t", "c1o", "c1t", "b1o", "b1t", "b2o", "b2t", "b3t", "d0t", "b3o", "d1t", "d0o", "d1o")
 SECOND = ("d1o", "d0o", "d1t", "d0t", "b3o", "b3t", "b2o", "b2t", "b1o", "b1t", "c1t", "c1o", "c0t", "c0o", "b0t", "b0o")
 BASE = {"b": 0, "c": 4, "d": 6}
 
@@ -107,13 +107,14 @@
 def kernel(lengths, q_hbm, pk_hbm, pv_hbm, rk_hbm, rv_hbm, g_hbm, dq_hbm, drk_hbm, drv_hbm, dpk_hbm, dpv_hbm,
            q, pk, pv, rk, rv, g, dq_out, drk, drv, dpk, dpv,
            qs, lives, peak, denom, weighted, peaks, exps, gprobs, dq, dq_send, dq_in,
-           stat_out, stat_in, packed, kv, own, half_out, half_in, ring_out, ring_in, z_out, z_in,
-           local_s, swap_s, swap_r, stat_s, stat_r, dq_s, dq_r, get_s, get_r, half_s, half_r, ring_s, ring_r, z_s, z_r):
+           stat_out, stat_in, packed, kv, own, ring_out, ring_in, z_out, z_in,
+           local_s, swap_s, swap_r, stat_s, stat_r, dq_s, dq_r, get_s, get_r, ring_s, ring_r, z_s, z_r):
     heads = q.shape[1] // HD
     resp, tensor = lax.axis_index("resp"), lax.axis_index("tensor")
     chip, core = resp // 2, resp % 2
     up = {"resp": (chip + 1) % 4 * 2 + core}
     down = {"resp": (chip + 3) % 4 * 2 + core}
+    across = {"resp": (chip + 2) % 4 * 2 + core}
     twin = {"resp": chip * 2 + 1 - core}
 
     def along(turn):
@@ -123,7 +124,7 @@
         return pl.ds(pl.multiple_of(index * HD, HD), HD)
 
     barrier = pltpu.get_barrier_semaphore()
-    for other in (up, down, twin, along(1), along(2), along(3)):
+    for other in (up, down, across, twin, along(1), along(2), along(3)):
         pl.semaphore_signal(barrier, inc=1, device_id=other, device_id_type=MESH)
     moves_in = [
         pltpu.make_async_copy(src, dst, local_s.at[i])
@@ -148,10 +149,8 @@
             ends = [(mine.at[part], kv.at[n, 0, part], up) for part in range(2)]
         elif kind == BEHIND:
             ends = [(mine.at[part], kv.at[n, 1, part], down) for part in range(2)]
-        elif kind == FAR_K:
-            ends = [(kv.at[n, 0, 0], far.at[0], up)]
         else:
-            ends = [(kv.at[n, 1, 1], far.at[1], down)]
+            ends = [(mine.at[part], far.at[part], across) for part in range(2)]
         return [send(src, dst, (get_s, get_r), (n, kind, i), to) for i, (src, dst, to) in enumerate(ends)]
 
     def start(copies):
@@ -165,14 +164,11 @@
     def begin(n):
         if n:
             received(get(n, SPREAD))
-        start(get(n, AHEAD))
-        start(get(n, BEHIND))
-
-    def forward(n):
-        received(get(n, AHEAD))
-        start(get(n, FAR_K))
-        received(get(n, BEHIND))
-        start(get(n, FAR_V))
+        for kind in (AHEAD, BEHIND, ACROSS):
+            start(get(n, kind))
+
+    def near_received(n):
+        received(get(n, AHEAD) + get(n, BEHIND))
 
     def swap():
         return [
@@ -191,7 +187,7 @@
         cols = columns((tensor + TURN[n]) % 4)
         packed[n, 0] = pk[:, cols]
         packed[n, 1] = pv[:, cols]
-    pl.semaphore_wait(barrier, 6)
+    pl.semaphore_wait(barrier, 7)
     begin(0)
     for n in range(1, ROUNDS):
         start(get(n, SPREAD))
@@ -216,19 +212,20 @@
 
     def far_received(*rounds):
         for n in rounds:
-            received(get(n, FAR_K) + get(n, FAR_V))
+            received(get(n, ACROSS))
 
     before = {
-        "b0o": (lambda: forward(0),),
+        "b0o": (lambda: near_received(0),),
         "b0t": (lambda: received(swap()),),
+        "b1o": (lambda: near_received(1),),
+        "b2o": (lambda: near_received(2),),
+        "b3t": (lambda: near_received(3),),
         "d0t": (lambda: far_received(0, 1),),
         "d1t": (lambda: far_received(2, 3),),
     }
     after = {
         "b0o": (lambda: begin(1), lambda: begin(2)),
         "c0t": (lambda: begin(3),),
-        "c1o": (lambda: forward(1), lambda: forward(2)),
-        "b2o": (lambda: forward(3),),
     }
 
     def serve(step, order, table):
@@ -262,14 +259,9 @@
     tell(1).wait_recv()
     finish_stats(0, heads, stat_out.at[0], stat_in.at[0], peak, weighted)
 
-    def to_half(n, part):
-        return send(half_out.at[n, part], half_in.at[n, part], (half_s, half_r), (n, part), (up, down)[part])
-
     def to_ring(n, way):
-        return [
-            send(ring_out.at[n, way, part], ring_in.at[n, way, part], (ring_s, ring_r), (n, way, part), (up, down)[way])
-            for part in range(2)
-        ]
+        to = (up, down, across)[way]
+        return [send(ring_out.at[n, way], ring_in.at[n, way], (ring_s, ring_r), (n, way), to)]
 
     def to_holder(n):
         return [
@@ -282,22 +274,19 @@
     def wide(ref):
         return ref.astype(jnp.float32)
 
-    def halves(n):
-        half_out[n] = own[place("d", n)].astype(jnp.bfloat16)
-        to_half(n, 0).start()
-        to_half(n, 1).start()
-
-    def relay(n):
+    def send_far(n):
+        ring_out[n, 2] = own[place("d", n)].astype(jnp.bfloat16)
+        start(to_ring(n, 2))
+
+    def send_near(n):
         for way in range(2):
-            to_half(n, way).wait_recv()
-            part = own[n, 1 - way]
-            ring_out[n, way, way] = (part[way] + wide(half_in[n, way])).astype(jnp.bfloat16)
-            ring_out[n, way, 1 - way] = part[1 - way].astype(jnp.bfloat16)
+            ring_out[n, way] = own[n, 1 - way].astype(jnp.bfloat16)
             start(to_ring(n, way))
 
     def total(n):
-        received(to_ring(n, 0) + to_ring(n, 1))
-        return own[place("c", n)] + wide(ring_in[n, 0]) + wide(ring_in[n, 1])
+        for way in range(3):
+            received(to_ring(n, way))
+        return own[place("c", n)] + wide(ring_in[n, 0]) + wide(ring_in[n, 1]) + wide(ring_in[n, 2])
 
     def hand_over(n):
         z_out[n] = total(n).astype(jnp.bfloat16)
@@ -314,14 +303,15 @@
 
     services = {
         "d0o": (learn,),
-        "d1t": (lambda: halves(3), lambda: halves(2)),
-        "d0t": (lambda: halves(1), lambda: halves(0)),
-        "b2t": (lambda: relay(3), lambda: relay(2)),
-        "b1t": (lambda: relay(1),),
+        "d1t": (lambda: send_far(3), lambda: send_far(2)),
+        "d0t": (lambda: send_far(1), lambda: send_far(0)),
+        "b3t": (lambda: send_near(3),),
+        "b2t": (lambda: send_near(2),),
+        "b1t": (lambda: send_near(1),),
         "c1o": (lambda: hand_over(3), lambda: hand_over(2)),
         "c0o": (lambda: hand_over(1),),
         "b0t": (return_queries,),
-        "b0o": (lambda: relay(0),),
+        "b0o": (lambda: send_near(0),),
     }
 
     def second(step, carry):
@@ -365,9 +355,9 @@
     moves_out[4].start()
     sent = swap() + [tell(0), tell(1)] + [to_owner(h) for h in range(heads)]
     for n in range(ROUNDS):
-        for kind in range(SPREAD if n else AHEAD, FAR_V + 1):
+        for kind in range(SPREAD if n else AHEAD, ACROSS + 1):
             sent += get(n, kind)
-        sent += [to_half(n, 0), to_half(n, 1)] + to_ring(n, 0) + to_ring(n, 1)
+        sent += to_ring(n, 0) + to_ring(n, 1) + to_ring(n, 2)
         if n:
             sent += to_holder(n)
     for copy in sent:
@@ -428,19 +418,16 @@
             pltpu.VMEM((ROUNDS,) + piece, bf16),
             pltpu.VMEM((2 * ROUNDS, 2) + piece, bf16),
             pltpu.VMEM((2 * ROUNDS, 2) + piece, f32),
-            pltpu.VMEM((ROUNDS,) + piece, bf16),
-            pltpu.VMEM((ROUNDS,) + piece, bf16),
-            pltpu.VMEM((ROUNDS, 2) + piece, bf16),
-            pltpu.VMEM((ROUNDS, 2) + piece, bf16),
+            pltpu.VMEM((ROUNDS, 3) + piece, bf16),
+            pltpu.VMEM((ROUNDS, 3) + piece, bf16),
             pltpu.VMEM((ROUNDS,) + piece, bf16),
             pltpu.VMEM((ROUNDS,) + piece, bf16),
             pltpu.SemaphoreType.DMA((11,)),
             *sems(2, heads),
             *sems(2),
             *sems(heads),
-            *sems(ROUNDS, 5, 2),
-            *sems(ROUNDS, 2),
-            *sems(ROUNDS, 2, 2),
+            *sems(ROUNDS, 4, 2),
+            *sems(ROUNDS, 3),
             *sems(ROUNDS, 2),
         ],
         compiler_params=pltpu.CompilerParams(

time: 54.3 us -> 53.8 us (level)
  the two profiles are of different devices: /device:TPU:8 before, /device:TPU:1 now
where the time goes in v9:
time: 53.8 us; the launch traced here: 53.7 us
  Pallas kernels  52.4 us (97%)
  between operations  1.29 us (2%)
    pallas_call x1, Pallas kernels, local(): pl.pallas_call(kernel, out_shape=outs, in_specs=[pl.BlockSpec(memory_spac...  50.1 us
    pallas_call x1, Pallas kernels, local(): pl.pallas_call(copy_kernel, out_shape=outs, in_specs=[anywhere] * 5, out_...  2.27 us

profile of v9, /device:TPU:1, one launch (start us, length us, event | category | flops | bytes accessed | tf_op | source)
XLA Modules:
  0.0 53.7 jit_solution(1729045051588263745)
XLA Ops:
  1.3 50.1 %shard_map.110 = (f32[256,640]{1,0:T(8,128)}, f32[256,128]{1,0:T(8,128)}, f32[256,128]{1,0:T(8,128)}, f32[128,512]{1,0:T(8,128)}, f32[128,512]{1,0:T(8,128)}) custom-call(s32[1]{0:T(128)S(6)} %copy.12.lengths, bf16[256,640]{1,0:T(8,128)(2,1)} %q_hbm.1, bf16[128,512]{1,0:T(8,128)(2,1)} %pk_hbm.1, bf16[128,512]{1,0:T(8,128)(2,1)} %pv_hbm.1, ...), custom_call_target="tpu_custom_call" | custom-call | flops 7130316800 | bytes 3145728 | tf_op jit(solution)/shard_map/pallas_call | solution.py:397
  51.4 2.3 %shard_map.111 = (f32[256,640]{1,0:T(8,128)}, f32[256,128]{1,0:T(8,128)}, f32[256,128]{1,0:T(8,128)}, f32[128,512]{1,0:T(8,128)}, f32[128,512]{1,0:T(8,128)}) custom-call(f32[256,640]{1,0:T(8,128)} %get-tuple-element.10.refs_0_, f32[256,128]{1,0:T(8,128)} %get-tuple-element.11.refs_1_, f32[256,128]{1,0:T(8,128)} %get-tuple-element.12.refs_2_, ...), custom_call_target="tpu_custom_call" | custom-call | tf_op jit(solution)/shard_map/pallas_call | solution.py:438

commit v10 on v9

--- a/solution.py
+++ b/solution.py
@@ -23,6 +23,7 @@
 MESH = pl.DeviceIdType.MESH
 QUARTER = 128
 ROUNDS = 4
+PIECES = 4
 TURN = (0, 1, 3, 2)
 SPREAD, AHEAD, BEHIND, ACROSS = range(4)
 
@@ -334,7 +335,7 @@
     moves_out = [
         pltpu.make_async_copy(src, dst, local_s.at[6 + i])
         for i, (src, dst) in enumerate((
-            (drk, drk_hbm), (drv, drv_hbm), (dq_out, dq_hbm), (dpk, dpk_hbm), (dpv, dpv_hbm)
+            (drk, drk_hbm), (drv, drv_hbm), (dq_out, dq_hbm)
         ))
     ]
     moves_out[0].start()
@@ -343,20 +344,26 @@
         to_owner(h).wait_recv()
         dq_out[:, h * HD : (h + 1) * HD] = (dq[h] + wide(dq_in[h])).T * SCALE
     moves_out[2].start()
-    sums_now = total(0)
-    dpk[:, columns(tensor)] = sums_now[0]
-    dpv[:, columns(tensor)] = sums_now[1]
-    for n in reversed(range(1, ROUNDS)):
-        received(to_holder(n))
-        cols = columns((tensor + TURN[n]) % 4)
-        dpk[:, cols] = wide(z_in[n, 0])
-        dpv[:, cols] = wide(z_in[n, 1])
-    moves_out[3].start()
-    moves_out[4].start()
-    sent = swap() + [tell(0), tell(1)] + [to_owner(h) for h in range(heads)]
+    sent = swap() + [tell(0), tell(1)]
     for n in range(ROUNDS):
         for kind in range(SPREAD if n else AHEAD, ACROSS + 1):
             sent += get(n, kind)
+    for copy in sent:
+        copy.wait_send()
+
+    def prompt_out(n, values):
+        cols = columns((tensor + TURN[n]) % 4)
+        for part, (here, there) in enumerate(((dpk, dpk_hbm), (dpv, dpv_hbm))):
+            here[:, cols] = values[part]
+            moves_out.append(pltpu.make_async_copy(here.at[:, cols], there.at[:, cols], local_s.at[9 + 2 * n + part]))
+            moves_out[-1].start()
+
+    prompt_out(0, total(0))
+    for n in reversed(range(1, ROUNDS)):
+        received(to_holder(n))
+        prompt_out(n, wide(z_in[n]))
+    sent = [to_owner(h) for h in range(heads)]
+    for n in range(ROUNDS):
         sent += to_ring(n, 0) + to_ring(n, 1) + to_ring(n, 2)
         if n:
             sent += to_holder(n)
@@ -369,14 +376,18 @@
 def copy_kernel(*refs):
     sems = refs[-1]
     count = (len(refs) - 1) // 3
-    ins, outs, rooms = refs[:count], refs[count : 2 * count], refs[2 * count : 3 * count]
-    here = [pltpu.make_async_copy(ins[i], rooms[i], sems.at[0, i]) for i in range(count)]
-    away = [pltpu.make_async_copy(rooms[i], outs[i], sems.at[1, i]) for i in range(count)]
+    here, away = [], []
+    for src, dst, room in zip(refs[:count], refs[count : 2 * count], refs[2 * count : 3 * count]):
+        step = src.shape[0] // PIECES
+        for i in range(PIECES):
+            rows, at = pl.ds(i * step, step), len(here)
+            here.append(pltpu.make_async_copy(src.at[rows], room.at[rows], sems.at[0, at]))
+            away.append(pltpu.make_async_copy(room.at[rows], dst.at[rows], sems.at[1, at]))
     for move in here:
         move.start()
-    for i in range(count):
-        here[i].wait()
-        away[i].start()
+    for move_in, move_out in zip(here, away):
+        move_in.wait()
+        move_out.start()
     for move in away:
         move.wait()
 
@@ -422,7 +433,7 @@
             pltpu.VMEM((ROUNDS, 3) + piece, bf16),
             pltpu.VMEM((ROUNDS,) + piece, bf16),
             pltpu.VMEM((ROUNDS,) + piece, bf16),
-            pltpu.SemaphoreType.DMA((11,)),
+            pltpu.SemaphoreType.DMA((17,)),
             *sems(2, heads),
             *sems(2),
             *sems(heads),
@@ -440,7 +451,7 @@
         out_shape=outs,
         in_specs=[anywhere] * 5,
         out_specs=[anywhere] * 5,
-        scratch_shapes=[pltpu.VMEM(x.shape, f32) for x in outs] + [pltpu.SemaphoreType.DMA((2, 5))],
+        scratch_shapes=[pltpu.VMEM(x.shape, f32) for x in outs] + [pltpu.SemaphoreType.DMA((2, 5 * PIECES))],
         compiler_params=pltpu.CompilerParams(vmem_limit_bytes=61 * 1024 * 1024),
     )(*results)
 

time: 53.8 us -> 53.9 us (level)
  no operation moved by 1% of the time
where the time goes in v10:
time: 53.9 us; the launch traced here: 53.8 us
  Pallas kernels  52.5 us (97%)
  between operations  1.29 us (2%)
    pallas_call x1, Pallas kernels, local(): pl.pallas_call(kernel, out_shape=outs, in_specs=[pl.BlockSpec(memory_spac...  50.1 us
    pallas_call x1, Pallas kernels, local(): pl.pallas_call(copy_kernel, out_shape=outs, in_specs=[anywhere] * 5, out_...  2.42 us

profile of v10, /device:TPU:1, one launch (start us, length us, event | category | flops | bytes accessed | tf_op | source)
XLA Modules:
  0.0 53.8 jit_solution(15773655481611164092)
XLA Ops:
  1.3 50.1 %shard_map.110 = (f32[256,640]{1,0:T(8,128)}, f32[256,128]{1,0:T(8,128)}, f32[256,128]{1,0:T(8,128)}, f32[128,512]{1,0:T(8,128)}, f32[128,512]{1,0:T(8,128)}) custom-call(s32[1]{0:T(128)S(6)} %copy.12.lengths, bf16[256,640]{1,0:T(8,128)(2,1)} %q_hbm.1, bf16[128,512]{1,0:T(8,128)(2,1)} %pk_hbm.1, bf16[128,512]{1,0:T(8,128)(2,1)} %pv_hbm.1, ...), custom_call_target="tpu_custom_call" | custom-call | flops 7130316800 | bytes 3145728 | tf_op jit(solution)/shard_map/pallas_call | solution.py:408
  51.4 2.4 %shard_map.111 = (f32[256,640]{1,0:T(8,128)}, f32[256,128]{1,0:T(8,128)}, f32[256,128]{1,0:T(8,128)}, f32[128,512]{1,0:T(8,128)}, f32[128,512]{1,0:T(8,128)}) custom-call(f32[256,640]{1,0:T(8,128)} %get-tuple-element.10.refs_0_, f32[256,128]{1,0:T(8,128)} %get-tuple-element.11.refs_1_, f32[256,128]{1,0:T(8,128)} %get-tuple-element.12.refs_2_, ...), custom_call_target="tpu_custom_call" | custom-call | tf_op jit(solution)/shard_map/pallas_call | solution.py:449

commit v11 on v9

--- a/solution.py
+++ b/solution.py
@@ -143,15 +143,13 @@
 
     def get(n, kind):
         mine, far = kv.at[*place("c", n)], kv.at[*place("d", n)]
-        if kind == SPREAD:
-            ends = [(packed.at[n, part], mine.at[part], along(TURN[n])) for part in range(2)]
-        elif kind == AHEAD:
-            ends = [(mine.at[part], kv.at[n, 0, part], up) for part in range(2)]
-        elif kind == BEHIND:
-            ends = [(mine.at[part], kv.at[n, 1, part], down) for part in range(2)]
-        else:
-            ends = [(mine.at[part], far.at[part], across) for part in range(2)]
-        return [send(src, dst, (get_s, get_r), (n, kind, i), to) for i, (src, dst, to) in enumerate(ends)]
+        src, dst, to = {
+            SPREAD: (packed.at[n], mine, along(TURN[n])),
+            AHEAD: (mine, kv.at[n, 0], up),
+            BEHIND: (mine, kv.at[n, 1], down),
+            ACROSS: (mine, far, across),
+        }[kind]
+        return [send(src, dst, (get_s, get_r), (n, kind), to)]
 
     def start(copies):
         for copy in copies:
@@ -171,11 +169,8 @@
         received(get(n, AHEAD) + get(n, BEHIND))
 
     def swap():
-        return [
-            send(ref.at[h], ref.at[heads + h], (swap_s, swap_r), (i, h), twin)
-            for h in range(heads)
-            for i, ref in enumerate((qs, lives))
-        ]
+        here, there = pl.ds(0, heads), pl.ds(heads, heads)
+        return [send(ref.at[here], ref.at[there], (swap_s, swap_r), i, twin) for i, ref in enumerate((qs, lives))]
 
     positions = lax.broadcasted_iota(jnp.int32, (ROWS, HD), 0)
     alive = positions < lengths[0]
@@ -264,12 +259,10 @@
         return [send(ring_out.at[n, way], ring_in.at[n, way], (ring_s, ring_r), (n, way), to)]
 
     def to_holder(n):
-        return [
-            send(z_out.at[n, part], z_in.at[n, part], (z_s, z_r), (n, part), along(4 - TURN[n])) for part in range(2)
-        ]
-
-    def to_owner(h):
-        return send(dq_send.at[h], dq_in.at[h], (dq_s, dq_r), h, twin)
+        return [send(z_out.at[n], z_in.at[n], (z_s, z_r), n, along(4 - TURN[n]))]
+
+    def to_owner():
+        return send(dq_send, dq_in, (dq_s, dq_r), 0, twin)
 
     def wide(ref):
         return ref.astype(jnp.float32)
@@ -299,7 +292,7 @@
     def return_queries():
         for h in range(heads):
             dq_send[h] = dq[heads + h].astype(jnp.bfloat16)
-            to_owner(h).start()
+        to_owner().start()
 
     services = {
         "d0o": (learn,),
@@ -339,8 +332,8 @@
     ]
     moves_out[0].start()
     moves_out[1].start()
+    to_owner().wait_recv()
     for h in range(heads):
-        to_owner(h).wait_recv()
         dq_out[:, h * HD : (h + 1) * HD] = (dq[h] + wide(dq_in[h])).T * SCALE
     moves_out[2].start()
     sums_now = total(0)
@@ -353,7 +346,7 @@
         dpv[:, cols] = wide(z_in[n, 1])
     moves_out[3].start()
     moves_out[4].start()
-    sent = swap() + [tell(0), tell(1)] + [to_owner(h) for h in range(heads)]
+    sent = swap() + [tell(0), tell(1), to_owner()]
     for n in range(ROUNDS):
         for kind in range(SPREAD if n else AHEAD, ACROSS + 1):
             sent += get(n, kind)
@@ -423,12 +416,12 @@
             pltpu.VMEM((ROUNDS,) + piece, bf16),
             pltpu.VMEM((ROUNDS,) + piece, bf16),
             pltpu.SemaphoreType.DMA((11,)),
-            *sems(2, heads),
             *sems(2),
-            *sems(heads),
-            *sems(ROUNDS, 4, 2),
+            *sems(2),
+            *sems(1),
+            *sems(ROUNDS, 4),
             *sems(ROUNDS, 3),
-            *sems(ROUNDS, 2),
+            *sems(ROUNDS),
         ],
         compiler_params=pltpu.CompilerParams(
             vmem_limit_bytes=61 * 1024 * 1024, collective_id=0, has_side_effects=True

time: 53.8 us -> 53.3 us (level)
  Pallas kernels: 52.4 us -> 51.8 us
    pallas_call x1, Pallas kernels: 50.1 us -> 49.6 us  [local(): pl.pallas_call(kernel, out_shape=outs, in_specs=[pl.BlockSpec(memory_spac...]
where the time goes in v11:
time: 53.3 us; the launch traced here: 53.1 us
  Pallas kernels  51.8 us (97%)
  between operations  1.29 us (2%)
    pallas_call x1, Pallas kernels, local(): pl.pallas_call(kernel, out_shape=outs, in_specs=[pl.BlockSpec(memory_spac...  49.6 us
    pallas_call x1, Pallas kernels, local(): pl.pallas_call(copy_kernel, out_shape=outs, in_specs=[anywhere] * 5, out_...  2.27 us

profile of v11, /device:TPU:1, one launch (start us, length us, event | category | flops | bytes accessed | tf_op | source)
XLA Modules:
  0.0 53.1 jit_solution(10443585190045270000)
XLA Ops:
  1.3 49.6 %shard_map.110 = (f32[256,640]{1,0:T(8,128)}, f32[256,128]{1,0:T(8,128)}, f32[256,128]{1,0:T(8,128)}, f32[128,512]{1,0:T(8,128)}, f32[128,512]{1,0:T(8,128)}) custom-call(s32[1]{0:T(128)S(6)} %copy.12.lengths, bf16[256,640]{1,0:T(8,128)(2,1)} %q_hbm.1, bf16[128,512]{1,0:T(8,128)(2,1)} %pk_hbm.1, bf16[128,512]{1,0:T(8,128)(2,1)} %pv_hbm.1, ...), custom_call_target="tpu_custom_call" | custom-call | flops 7130316800 | bytes 3145728 | tf_op jit(solution)/shard_map/pallas_call | solution.py:390
  50.9 2.3 %shard_map.111 = (f32[256,640]{1,0:T(8,128)}, f32[256,128]{1,0:T(8,128)}, f32[256,128]{1,0:T(8,128)}, f32[128,512]{1,0:T(8,128)}, f32[128,512]{1,0:T(8,128)}) custom-call(f32[256,640]{1,0:T(8,128)} %get-tuple-element.10.refs_0_, f32[256,128]{1,0:T(8,128)} %get-tuple-element.11.refs_1_, f32[256,128]{1,0:T(8,128)} %get-tuple-element.12.refs_2_, ...), custom_call_target="tpu_custom_call" | custom-call | tf_op jit(solution)/shard_map/pallas_call | solution.py:431

commit v12 on v11

--- a/solution.py
+++ b/solution.py
@@ -26,8 +26,8 @@
 TURN = (0, 1, 3, 2)
 SPREAD, AHEAD, BEHIND, ACROSS = range(4)
 
-FIRST = ("b0o", "c0o", "b0t", "c0t", "c1o", "c1t", "b1o", "b1t", "b2o", "b2t", "b3t", "d0t", "b3o", "d1t", "d0o", "d1o")
-SECOND = ("d1o", "d0o", "d1t", "d0t", "b3o", "b3t", "b2o", "b2t", "b1o", "b1t", "c1t", "c1o", "c0t", "c0o", "b0t", "b0o")
+FIRST = ("b0o", "c0o", "b0t", "c0t", "c1o", "c1t", "b1o", "b1t", "b2o", "b2t", "b3t", "d0t", "d1t", "b3o", "d0o", "d1o")
+SECOND = ("d1o", "d0o", "b3o", "d1t", "d0t", "b3t", "b2o", "b2t", "b1o", "b1t", "c1t", "c1o", "c0t", "c0o", "b0t", "b0o")
 BASE = {"b": 0, "c": 4, "d": 6}
 
 
@@ -295,7 +295,7 @@
         to_owner().start()
 
     services = {
-        "d0o": (learn,),
+        "b3o": (learn,),
         "d1t": (lambda: send_far(3), lambda: send_far(2)),
         "d0t": (lambda: send_far(1), lambda: send_far(0)),
         "b3t": (lambda: send_near(3),),

time: 53.3 us -> 52.8 us (level)
  no operation moved by 1% of the time
where the time goes in v12:
time: 52.8 us; the launch traced here: 52.7 us
  Pallas kernels  51.4 us (97%)
  between operations  1.29 us (2%)
    pallas_call x1, Pallas kernels, local(): pl.pallas_call(kernel, out_shape=outs, in_specs=[pl.BlockSpec(memory_spac...  49.2 us
    pallas_call x1, Pallas kernels, local(): pl.pallas_call(copy_kernel, out_shape=outs, in_specs=[anywhere] * 5, out_...  2.27 us

profile of v12, /device:TPU:1, one launch (start us, length us, event | category | flops | bytes accessed | tf_op | source)
XLA Modules:
  0.0 52.7 jit_solution(6177052405688048293)
XLA Ops:
  1.3 49.2 %shard_map.110 = (f32[256,640]{1,0:T(8,128)}, f32[256,128]{1,0:T(8,128)}, f32[256,128]{1,0:T(8,128)}, f32[128,512]{1,0:T(8,128)}, f32[128,512]{1,0:T(8,128)}) custom-call(s32[1]{0:T(128)S(6)} %copy.12.lengths, bf16[256,640]{1,0:T(8,128)(2,1)} %q_hbm.1, bf16[128,512]{1,0:T(8,128)(2,1)} %pk_hbm.1, bf16[128,512]{1,0:T(8,128)(2,1)} %pv_hbm.1, ...), custom_call_target="tpu_custom_call" | custom-call | flops 7130316800 | bytes 3145728 | tf_op jit(solution)/shard_map/pallas_call | solution.py:390
  50.4 2.3 %shard_map.111 = (f32[256,640]{1,0:T(8,128)}, f32[256,128]{1,0:T(8,128)}, f32[256,128]{1,0:T(8,128)}, f32[128,512]{1,0:T(8,128)}, f32[128,512]{1,0:T(8,128)}) custom-call(f32[256,640]{1,0:T(8,128)} %get-tuple-element.10.refs_0_, f32[256,128]{1,0:T(8,128)} %get-tuple-element.11.refs_1_, f32[256,128]{1,0:T(8,128)} %get-tuple-element.12.refs_2_, ...), custom_call_target="tpu_custom_call" | custom-call | tf_op jit(solution)/shard_map/pallas_call | solution.py:431

commit v13 on v12

--- a/solution.py
+++ b/solution.py
@@ -26,7 +26,7 @@
 TURN = (0, 1, 3, 2)
 SPREAD, AHEAD, BEHIND, ACROSS = range(4)
 
-FIRST = ("b0o", "c0o", "b0t", "c0t", "c1o", "c1t", "b1o", "b1t", "b2o", "b2t", "b3t", "d0t", "d1t", "b3o", "d0o", "d1o")
+FIRST = ("b0o", "c0o", "b0t", "c0t", "c1o", "c1t", "b1o", "b1t", "b2t", "b3t", "d0t", "d1t", "b2o", "b3o", "d0o", "d1o")
 SECOND = ("d1o", "d0o", "b3o", "d1t", "d0t", "b3t", "b2o", "b2t", "b1o", "b1t", "c1t", "c1o", "c0t", "c0o", "b0t", "b0o")
 BASE = {"b": 0, "c": 4, "d": 6}
 
@@ -183,9 +183,9 @@
         packed[n, 0] = pk[:, cols]
         packed[n, 1] = pv[:, cols]
     pl.semaphore_wait(barrier, 7)
-    begin(0)
     for n in range(1, ROUNDS):
         start(get(n, SPREAD))
+    begin(0)
     moves_in[2].wait()
     moves_in[3].wait()
     for h in range(heads):
@@ -213,7 +213,7 @@
         "b0o": (lambda: near_received(0),),
         "b0t": (lambda: received(swap()),),
         "b1o": (lambda: near_received(1),),
-        "b2o": (lambda: near_received(2),),
+        "b2t": (lambda: near_received(2),),
         "b3t": (lambda: near_received(3),),
         "d0t": (lambda: far_received(0, 1),),
         "d1t": (lambda: far_received(2, 3),),

time: 52.8 us -> 53.6 us (1.015)
  Pallas kernels: 51.4 us -> 52.2 us
    pallas_call x1, Pallas kernels: 49.2 us -> 49.9 us  [local(): pl.pallas_call(kernel, out_shape=outs, in_specs=[pl.BlockSpec(memory_spac...]
where the time goes in v13:
time: 53.6 us; the launch traced here: 53.5 us
  Pallas kernels  52.2 us (97%)
  between operations  1.29 us (2%)
    pallas_call x1, Pallas kernels, local(): pl.pallas_call(kernel, out_shape=outs, in_specs=[pl.BlockSpec(memory_spac...  49.9 us
    pallas_call x1, Pallas kernels, local(): pl.pallas_call(copy_kernel, out_shape=outs, in_specs=[anywhere] * 5, out_...  2.27 us

profile of v13, /device:TPU:1, one launch (start us, length us, event | category | flops | bytes accessed | tf_op | source)
XLA Modules:
  0.0 53.5 jit_solution(3622300197887704363)
XLA Ops:
  1.3 49.9 %shard_map.110 = (f32[256,640]{1,0:T(8,128)}, f32[256,128]{1,0:T(8,128)}, f32[256,128]{1,0:T(8,128)}, f32[128,512]{1,0:T(8,128)}, f32[128,512]{1,0:T(8,128)}) custom-call(s32[1]{0:T(128)S(6)} %copy.12.lengths, bf16[256,640]{1,0:T(8,128)(2,1)} %q_hbm.1, bf16[128,512]{1,0:T(8,128)(2,1)} %pk_hbm.1, bf16[128,512]{1,0:T(8,128)(2,1)} %pv_hbm.1, ...), custom_call_target="tpu_custom_call" | custom-call | flops 7130316800 | bytes 3145728 | tf_op jit(solution)/shard_map/pallas_call | solution.py:390
  51.2 2.3 %shard_map.111 = (f32[256,640]{1,0:T(8,128)}, f32[256,128]{1,0:T(8,128)}, f32[256,128]{1,0:T(8,128)}, f32[128,512]{1,0:T(8,128)}, f32[128,512]{1,0:T(8,128)}) custom-call(f32[256,640]{1,0:T(8,128)} %get-tuple-element.10.refs_0_, f32[256,128]{1,0:T(8,128)} %get-tuple-element.11.refs_1_, f32[256,128]{1,0:T(8,128)} %get-tuple-element.12.refs_2_, ...), custom_call_target="tpu_custom_call" | custom-call | tf_op jit(solution)/shard_map/pallas_call | solution.py:431
